TPU v7x, 128 devices: a whole 4x4x4 slice. The times are simulated.
128 devices in a mesh: line: 8 (over y, core), track: 16 (over x, z).
Axes of the slice: x: 4, y: 4, z: 4, core: 2. Of those that a mesh axis runs over, the one named last changes fastest.
Arguments:
- radiance: bfloat16 [8, 425, 256, 384], P('line', None, 'track')
- counts: int32 [8, 16], P('line', 'track'), may hold values from 4 to 16, as said below
- start: float32 [425, 64], replicated, may hold values from -0.3125 to 0.3125
Outputs:
- projector: float32 [425, 425], replicated
- scores: float32 [8, 64, 256, 384], P('line', None, 'track')
Inputs may be any that keep to these rules, and one draw needn't show every extreme that they name: `counts`: every tile has at least 4 valid rows, and at least one tile is wholly valid.
All inputs are finite; a program needn't handle non-finite values.
Results may differ from a plain program's by a relative error of at most 0.0024.
The roundings to bfloat16 on the way count: a program that leaves them out, or rounds other values in their place, can miss the bound.
Values may be sent and summed in bfloat16 or wider, within the bound.
A program may use at most 128 MiB of HBM per device.

v0:
```python
import jax
import jax.numpy as jnp
from jax import lax
from jax.sharding import PartitionSpec as P

ITERS = 6


def extended(x, sides, width):
    for axis, dim in sides:
        size, length = (lax.axis_size(axis), x.shape[dim])
        up = [(i, (i + 1) % size) for i in range(size - 1)]
        down = [(j, i) for i, j in up]
        last = lax.slice_in_dim(x, length - width, length, axis=dim)
        first = lax.slice_in_dim(x, 0, width, axis=dim)
        before = lax.ppermute(last, axis, up)
        after = lax.ppermute(first, axis, down)
        x = jnp.concatenate([before, x, after], axis=dim)
    return x


def make_features(padded, valid):
    rows_out = padded.shape[1] - 4
    smooth = (
        padded[:, 0:rows_out]
        + 4.0 * padded[:, 1 : rows_out + 1]
        + 6.0 * padded[:, 2 : rows_out + 2]
        + 4.0 * padded[:, 3 : rows_out + 3]
        + padded[:, 4 : rows_out + 4]
    ) / 16.0
    cols_out = smooth.shape[2]
    wide = jnp.pad(smooth, ((0, 0), (0, 0), (2, 2)))
    smooth = (
        wide[:, :, 0:cols_out]
        + 4.0 * wide[:, :, 1 : cols_out + 1]
        + 6.0 * wide[:, :, 2 : cols_out + 2]
        + 4.0 * wide[:, :, 3 : cols_out + 3]
        + wide[:, :, 4 : cols_out + 4]
    ) / 16.0
    banded = jnp.pad(smooth, ((1, 1), (0, 0), (0, 0)))
    derived = 0.5 * (banded[2:] - banded[:-2]) * valid[None, :, None]
    return derived.astype(jnp.bfloat16).reshape(derived.shape[0], -1)


def orthonormal(block):
    inner = jnp.dot(block.T, block, precision=lax.Precision.HIGHEST)
    factor = jnp.linalg.cholesky(inner)
    return lax.linalg.triangular_solve(factor, block, left_side=False, lower=True, transpose_a=True)


def on_device(radiance, counts, start):
    tile_rows = radiance.shape[2]
    tile_cols = radiance.shape[3]
    valid_rows = lax.iota(jnp.int32, tile_rows) < counts[0, 0]
    masked = radiance * valid_rows.astype(jnp.bfloat16)[None, None, :, None]
    padded = extended(masked, (("track", 2),), 2)
    features = make_features(padded[0].astype(jnp.float32), valid_rows.astype(jnp.float32))
    basis = orthonormal(start)
    for iteration in range(ITERS):
        coords = jnp.dot(
            basis.T, features, precision=lax.Precision.HIGHEST, preferred_element_type=jnp.float32
        )
        image = jnp.dot(
            features, coords.T, precision=lax.Precision.HIGHEST, preferred_element_type=jnp.float32
        )
        summed = lax.psum(image, ("line", "track"))
        basis = orthonormal(summed)
    projector = jnp.dot(basis, basis.T, precision=lax.Precision.HIGHEST)
    narrow = basis.astype(jnp.bfloat16)
    scores = jnp.dot(narrow.T, features, preferred_element_type=jnp.float32)
    return (projector, scores.reshape(1, narrow.shape[1], tile_rows, tile_cols))


def solution(mesh):
    return jax.shard_map(
        on_device,
        mesh=mesh,
        in_specs=(P("line", None, "track", None), P("line", "track"), P()),
        out_specs=(P(), P("line", None, "track", None)),
        check_vma=False,
    )
```

profile of v0, /device:TPU:1, one launch (start us, length us, event | category | flops | bytes accessed | tf_op | source)
XLA Modules:
  0.0 1106.9 jit_solution(16769854183955519764)
XLA Ops:
  7.9 4.3 copy_multiply_fusion
  12.2 2.3 copy-done.4
  14.6 4.4 collective-permute-start
  20.7 5.8 cholesky.119
  27.9 4.9 custom-call.11
  33.2 3.6 collective-permute-done.1
  36.7 7.7 fusion.10
  44.4 25.5 %broadcast_multiply_fusion = (f32[425,16,384]{2,0,1:T(8,128)}, f32[425,16,384]{2,0,1:T(8,128)}) fusion(f32[425,20,384]{2,0,1:T(8,128)} %fusion.10), kind=kLoop, calls=%fused_computation.24 | loop fusion | flops 20889600 | bytes 73113600 | tf_op jit(solution)/shard_map/div | solution.py:24
  69.9 24.6 %fusion.4 = f32[425,16,384]{2,0,1:T(8,128)} fusion(f32[425,16,384]{2,0,1:T(8,128)} %get-tuple-element.12, f32[425,16,384]{2,0,1:T(8,128)} %get-tuple-element.13), kind=kLoop, calls=%fused_computation.8 | loop fusion | flops 20889600 | bytes 31334400 | tf_op jit(solution)/shard_map/div | solution.py:33
  94.5 8.6 multiply_convert_fusion
  104.7 1.8 copy-done.3
  106.5 1.8 copy.43
  108.3 2.9 fusion.53
  111.2 5.3 fusion.54
  116.6 143.9 %all-reduce.9.cloned.1.call-done = f32[425,64]{0,1:T(8,128)} async-done(((f32[425,64]{0,1:T(8,128)}), f32[425,64]{0,1:T(8,128)}) %all-reduce.9.cloned.1.call-update) | async-done | bytes 108816 | tf_op jit(solution)/shard_map/psum | solution.py:66
  261.8 5.8 cholesky.130
  269.0 4.9 custom-call.12
  273.9 1.4 convolution_bitcast_fusion.5
  275.3 5.2 fusion.56
  280.5 5.3 fusion.57
  285.9 137.5 %all-reduce.11.cloned.1.call-done = f32[425,64]{0,1:T(8,128)} async-done(((f32[425,64]{0,1:T(8,128)}), f32[425,64]{0,1:T(8,128)}) %all-reduce.11.cloned.1.call-update) | async-done | bytes 108816 | tf_op jit(solution)/shard_map/psum | solution.py:66
  424.8 5.8 cholesky.141
  432.1 4.9 custom-call.13
  438.2 4.9 fusion.59
  443.2 5.4 fusion.60
  448.8 137.4 %all-reduce.13.cloned.1.call-done = f32[425,64]{0,1:T(8,128)} async-done(((f32[425,64]{0,1:T(8,128)}), f32[425,64]{0,1:T(8,128)}) %all-reduce.13.cloned.1.call-update) | async-done | bytes 108816 | tf_op jit(solution)/shard_map/psum | solution.py:66
  586.2 1.3 fusion.61
  587.6 5.8 cholesky.152
  594.8 4.9 custom-call.14
  600.9 4.9 fusion.62
  605.9 5.4 fusion.63
  611.5 137.4 %all-reduce.15.cloned.1.call-done = f32[425,64]{0,1:T(8,128)} async-done(((f32[425,64]{0,1:T(8,128)}), f32[425,64]{0,1:T(8,128)}) %all-reduce.15.cloned.1.call-update) | async-done | bytes 108816 | tf_op jit(solution)/shard_map/psum | solution.py:66
  750.3 5.8 cholesky.163
  757.5 4.9 custom-call.15
  763.7 4.9 fusion.65
  768.6 5.4 fusion.66
  774.1 137.6 %all-reduce.17.cloned.1.call-done = f32[425,64]{0,1:T(8,128)} async-done(((f32[425,64]{0,1:T(8,128)}), f32[425,64]{0,1:T(8,128)}) %all-reduce.17.cloned.1.call-update) | async-done | bytes 108816 | tf_op jit(solution)/shard_map/psum | solution.py:66
  913.0 5.8 cholesky.174
  920.2 4.9 custom-call.16
  926.3 5.0 fusion.68
  931.3 7.9 fusion.69
  939.2 5.3 slice_bitcast_fusion
  944.6 132.3 %all-reduce.19.cloned.1.call-done = f32[425,64]{0,1:T(8,128)} async-done(((f32[425,64]{0,1:T(8,128)}), f32[425,64]{0,1:T(8,128)}) %all-reduce.19.cloned.1.call-update) | async-done | bytes 108816 | tf_op jit(solution)/shard_map/psum | solution.py:66
  1078.2 5.8 cholesky.185
  1085.4 4.9 custom-call.17
  1091.5 1.8 fusion.71
  1093.3 4.2 fusion.13
  1097.6 2.1 copy.42
  (94 shorter events, 26.9 us)
Async XLA Ops:
  7.2 13.2 %copy-start = (f32[425,64]{0,1:T(8,128)S(1)}, f32[425,64]{0,1:T(8,128)}, u32[]{:S(2)}) copy-start(f32[425,64]{0,1:T(8,128)} %param.8) | copy-start | bytes 326404
  7.2 253.3 %all-reduce.9.cloned.1.call-start = ((), (), s32[]{:S(2)}) async-start(), calls=%async_computation | async-start | bytes 262144 | tf_op jit(solution)/shard_map/psum | solution.py:66
  12.2 2.3 copy-start.4
  14.6 18.5 %collective-permute-start = (bf16[1,425,2,384]{3,1,2,0:T(8,128)(2,1)S(1)}, bf16[1,425,2,384]{3,1,2,0:T(8,128)(2,1)S(1)}, u32[]{:S(2)}, u32[]{:S(2)}) collective-permute-start(bf16[1,425,2,384]{3,1,2,0:T(8,128)(2,1)S(1)} %get-tuple-element.14), channel_id=1, source_target_pairs={{0,1},{1,2},{2,3},{3,4},{4,5},{5,6},{6,7},{7,8},{8,9},{9,10},{10,1... | collective-permute-start | bytes 1958408 | tf_op jit(solution)/shard_map/ppermute | solution.py:16
  19.1 17.7 %collective-permute-start.1 = (bf16[1,425,2,384]{3,1,2,0:T(8,128)(2,1)S(1)}, bf16[1,425,2,384]{3,1,2,0:T(8,128)(2,1)S(1)}, u32[]{:S(2)}, u32[]{:S(2)}) collective-permute-start(bf16[1,425,2,384]{3,1,2,0:T(8,128)(2,1)S(1)} %get-tuple-element.15), channel_id=1, source_target_pairs={{1,0},{2,1},{3,2},{4,3},{5,4},{6,5},{7,6},{8,7},{9,8},{10,9},{11,1... | collective-permute-start | bytes 1958408 | tf_op jit(solution)/shard_map/ppermute | solution.py:17
  104.2 2.3 copy-start.3
  108.3 2.9 copy-start.2
  116.6 306.9 %all-reduce.11.cloned.1.call-start = ((), (), s32[]{:S(2)}) async-start(), calls=%async_computation.1 | async-start | bytes 262144 | tf_op jit(solution)/shard_map/psum | solution.py:66
  273.9 6.6 slice-start
  275.3 5.2 slice-start.1
  285.9 300.3 %all-reduce.13.cloned.1.call-start = ((), (), s32[]{:S(2)}) async-start(), calls=%async_computation.2 | async-start | bytes 262144 | tf_op jit(solution)/shard_map/psum | solution.py:66
  431.3 11.8 %slice-start.2 = ((s8[5308416]{0:T(1024)(128)(4,1)}), s8[1114112]{0:T(1024)(128)(4,1)S(1)}, s32[]{:S(2)}) async-start(s8[5308416]{0:T(1024)(128)(4,1)} %bitcast.160), calls=%async_computation.8 | async-start | bytes 2228224
  438.2 5.0 slice-start.3
  448.6 300.3 %all-reduce.15.cloned.1.call-start = ((), (), s32[]{:S(2)}) async-start(), calls=%async_computation.3 | async-start | bytes 262144 | tf_op jit(solution)/shard_map/psum | solution.py:66
  586.2 19.7 %slice-start.4 = ((s8[5308416]{0:T(1024)(128)(4,1)}), s8[1114112]{0:T(1024)(128)(4,1)S(1)}, s32[]{:S(2)}) async-start(s8[5308416]{0:T(1024)(128)(4,1)} %bitcast.163), calls=%async_computation.10 | async-start | bytes 2228224
  600.9 5.0 slice-start.5
  611.3 300.3 %all-reduce.17.cloned.1.call-start = ((), (), s32[]{:S(2)}) async-start(), calls=%async_computation.4 | async-start | bytes 262144 | tf_op jit(solution)/shard_map/psum | solution.py:66
  748.9 19.7 %slice-start.6 = ((s8[5308416]{0:T(1024)(128)(4,1)}), s8[1114112]{0:T(1024)(128)(4,1)S(1)}, s32[]{:S(2)}) async-start(s8[5308416]{0:T(1024)(128)(4,1)} %bitcast.166), calls=%async_computation.12 | async-start | bytes 2228224
  763.7 5.0 slice-start.7
  774.0 302.8 %all-reduce.19.cloned.1.call-start = ((), (), s32[]{:S(2)}) async-start(), calls=%async_computation.5 | async-start | bytes 262144 | tf_op jit(solution)/shard_map/psum | solution.py:66
  1091.5 8.1 copy-start.1
Sparse Core Ops, SparseCore 0:
  116.7 143.7 all-reduce.8
  286.0 137.4 all-reduce.10
  448.7 137.4 all-reduce.12
  611.4 137.4 all-reduce.14
  774.1 137.4 all-reduce.16
  939.4 137.4 all-reduce.18
where the time goes:
time: 1120 us; the launch traced here: 1110 us
  waiting for transfers between devices  830 us (74%)
  other arithmetic  155 us (14%)
  matrix products  84.3 us (8%)
  between operations  15.8 us (1%)
  local copies, waits for them, and re-layouts  15.6 us (1%)
    psum x6, waiting for transfers between devices, on_device(): summed = lax.psum(image, ('line', 'track'))  826 us
    another operation x21, other arithmetic, orthonormal(): factor = jnp.linalg.cholesky(inner)  45.6 us
    another operation x14, other arithmetic, orthonormal(): lax.linalg.triangular_solve(factor, block, left_side=False, lower=True, t...  38.9 us
    dot_general x6, matrix products, on_device(): jnp.dot(features, coords.T, precision=lax.Precision.HIGHEST, preferred_el...  34.6 us
    dot_general x6, matrix products, on_device(): jnp.dot(basis.T, features, precision=lax.Precision.HIGHEST, preferred_ele...  27.9 us
    div x1, other arithmetic, make_features(): (padded[:, 0:rows_out] + 4.0 * padded[:, 1:rows_out + 1] + 6.0 * padded[:...  25.5 us
    div x1, other arithmetic, make_features(): (wide[:, :, 0:cols_out] + 4.0 * wide[:, :, 1:cols_out + 1] + 6.0 * wide[:...  24.6 us
  transfers between devices with their start and end apart: 8, of which 7 were waited for; matrix products, arithmetic and copies ran while one was open for 2% of the time, Pallas kernels for 0%

commit v1 on v0

v1 whole, which is shorter than its diff:
```python
import functools

import jax
import jax.numpy as jnp
from jax import lax
from jax.experimental import pallas as pl
from jax.experimental.pallas import tpu as pltpu
from jax.sharding import PartitionSpec as P

MESH = pl.DeviceIdType.MESH
F32 = jnp.float32
BF16 = jnp.bfloat16

BANDS = 425
BP = 432
GROUPS = BP // 16
RANK = 64
ITERS = 6
ROWS = 16
COLS = 384
TILES = 16
CHUNK = 3
CHUNKS = GROUPS // CHUNK
HR = 16 + 2 * BP + 16
EDGE = (0, 1, 14, 15)
BIN = lambda dist: jnp.where(dist == 0, 6.0, jnp.where(dist == 1, 4.0, jnp.where(dist == 2, 1.0, 0.0)))
NT = (((1,), (1,)), ((), ()))
LOWER = [(rt, ct) for ct in range(4) for rt in range(16 * ct, BP // 8)]


def iotas(shape):
    return lax.broadcasted_iota(jnp.int32, shape, 0), lax.broadcasted_iota(jnp.int32, shape, 1)


def smooth_cols(t):
    rows = t.shape[0]
    lane = lax.broadcasted_iota(jnp.int32, (rows, 128), 1)
    first, last = lane == 0, lane == 127
    x = [t[:, 128 * i : 128 * i + 128] for i in range(3)]

    def right(v, edge):
        r = [pltpu.roll(a, 1, 1) for a in v]
        return [jnp.where(first, p, a) for p, a in zip([edge] + r[:2], r)]

    def left(v, edge):
        r = [pltpu.roll(a, 127, 1) for a in v]
        return [jnp.where(last, n, a) for n, a in zip(r[1:] + [edge], r)]

    zero = jnp.zeros((rows, 128), F32)
    v = [a + b for a, b in zip(x, right(x, zero))]
    y = [a + b for a, b in zip(v, left(v, x[2]))]
    w = [a + b for a, b in zip(y, right(y, x[0]))]
    return [a + b for a, b in zip(w, left(w, x[2] + y[2]))]


def features_kernel(
    counts_ref, x_hbm, f_hbm, g_ref,
    xs, su, sd, hu, hd, fs, tb, gs, pk, r1, r2, ag,
    x_sem, f_sem, su_sem, sd_sem, hu_sem, hd_sem, ex_send, ex_recv,
):
    line, track = lax.axis_index("line"), lax.axis_index("track")
    y, core = line // 2, line % 2
    xx, z = track // 4, track % 4
    chip = 16 * xx + 4 * y + z
    sibling = (2 * y + 1 - core, track)

    def peer(d):
        px, py, pz = (xx + d // 16) % 4, (y + (d // 4) % 4) % 4, (z + d % 4) % 4
        return 16 * px + 4 * py + pz, (2 * py + core, 4 * px + pz)

    crow = 256 * CHUNK

    def load(j):
        n = crow if j < CHUNKS - 1 else ROWS * BANDS - crow * (CHUNKS - 1)
        return pltpu.make_async_copy(
            x_hbm.at[pl.ds(crow * j, n)], xs.at[pl.ds(16 + crow * j, n)], x_sem.at[j]
        )

    for j in range(CHUNKS):
        load(j).start()

    barrier = pltpu.get_barrier_semaphore()
    pl.semaphore_signal(barrier, inc=1, device_id=sibling, device_id_type=MESH)

    def greet(d, carry):
        pl.semaphore_signal(barrier, inc=1, device_id=peer(d)[1], device_id_type=MESH)
        return carry

    lax.fori_loop(1, 64, greet, 0)

    xs[0:16, :] = jnp.zeros((16, COLS), BF16)
    tail = ROWS * (BANDS + 1)
    xs[tail : ROWS * (BP + 2), :] = jnp.zeros((ROWS * (BP + 2) - tail, COLS), BF16)
    for h in (hu, hd):
        h[0:16, :] = jnp.zeros((16, COLS), BF16)
        h[HR - 16 : HR, :] = jnp.zeros((16, COLS), BF16)
    gs[:, 384:512] = jnp.zeros((BP, 128), F32)

    cnt = counts_ref[0, 0]
    ri, ci = iotas((64, 256))
    want = jnp.where(ri < 32, ri & 1, 14 + (ri & 1))
    sel = ((((ri & 31) >> 1) == (ci >> 4)) & (want == (ci & 15)) & (want < cnt)).astype(F32).astype(BF16)

    ri, ci = iotas((128, 160))
    r, b, bi, rr = ri >> 3, ri & 7, ci >> 4, ci & 15
    sign = (bi == b + 2).astype(F32) - (bi == b).astype(F32)
    wt = jnp.where((r < cnt) & (rr < cnt), BIN(jnp.abs(rr - r)), 0.0)
    body = (sign * wt * (1.0 / 512.0)).astype(BF16)

    ri, ci = iotas((64, 128))
    q, b = ri >> 4, ri & 15
    r = jnp.where(q < 2, q, q + 12)
    up = ci < 64
    cj = ci & 63
    bi, rr = cj >> 1, jnp.where(up, (cj & 1) - 2, (cj & 1) + 16)
    sign = (bi == b + 9).astype(F32) - (bi == b + 7).astype(F32)
    have = jnp.where(up, track, TILES - 1 - track) > 0
    wt = jnp.where((r < cnt) & have, BIN(jnp.abs(rr - r)), 0.0)
    rim = (sign * wt * (1.0 / 512.0)).astype(BF16)

    def halo(j):
        rows = pl.ds(pl.multiple_of(16 + 32 * CHUNK * j, 32 * CHUNK // 6), 32 * CHUNK)
        first = pltpu.make_async_remote_copy(
            src_ref=su.at[rows], dst_ref=hd.at[rows], send_sem=su_sem.at[j], recv_sem=hd_sem.at[j],
            device_id=(line, (track + TILES - 1) % TILES), device_id_type=MESH,
        )
        last = pltpu.make_async_remote_copy(
            src_ref=sd.at[rows], dst_ref=hu.at[rows], send_sem=sd_sem.at[j], recv_sem=hu_sem.at[j],
            device_id=(line, (track + 1) % TILES), device_id_type=MESH,
        )
        return first, last

    for j in range(CHUNKS):
        load(j).wait()
        for g in range(CHUNK * j, CHUNK * j + CHUNK):
            picked = jnp.dot(sel, xs[16 + 256 * g : 272 + 256 * g, :], preferred_element_type=F32).astype(BF16)
            su[16 + 32 * g : 48 + 32 * g, :] = picked[0:32]
            sd[16 + 32 * g : 48 + 32 * g, :] = picked[32:64]
        if j == 0:
            pl.semaphore_wait(barrier, 64)
        for copy in halo(j):
            copy.start()

    def interior(g):
        at = pl.multiple_of(16 * g, 16)
        halves = []
        for h in range(2):
            xk = xs[pl.ds(pl.multiple_of(256 * g + 128 * h, 128), 160), :]
            t = jnp.dot(body, xk, preferred_element_type=F32)
            for e, row in enumerate(EDGE):
                tb[e, pl.ds(pl.multiple_of(at + 8 * h, 8), 8), :] = t[8 * row : 8 * row + 8]
            halves.append(smooth_cols(t[16:112]))
        for row in range(2, 14):
            k = 8 * (row - 2)
            for i in range(3):
                both = jnp.concatenate([halves[0][i][k : k + 8], halves[1][i][k : k + 8]], axis=0)
                col = row * COLS + 128 * i
                fs[pl.ds(at, 16), col : col + 128] = both.astype(BF16)

    def interior_step(s, carry):
        for u in range(3):
            interior(3 * s + u)
        return carry

    lax.fori_loop(0, GROUPS // 3, interior_step, 0)

    def outer(lo, hi):
        a = fs[:, lo:hi]
        left = lax.dot_general(a, a[0:256], NT, preferred_element_type=F32)
        right = lax.dot_general(a[256:BP], a[256:BP], NT, preferred_element_type=F32)
        return left, right

    left, right = outer(2 * COLS, 6 * COLS)
    gs[:, 0:256] = left
    gs[256:BP, 256:BP] = right
    for k in (6, 10):
        left, right = outer(k * COLS, (k + 4) * COLS)
        gs[:, 0:256] += left
        gs[256:BP, 256:BP] += right

    def edge(g):
        at = pl.multiple_of(16 * g, 16)
        src = pl.ds(pl.multiple_of(32 * g, 32), 64)
        halos = jnp.concatenate([hu[src, :], hd[src, :]], axis=0)
        t = jnp.dot(rim, halos, preferred_element_type=F32) + tb[:, pl.ds(at, 16), :].reshape(64, COLS)
        out = smooth_cols(t)
        for e, row in enumerate(EDGE):
            for i in range(3):
                col = row * COLS + 128 * i
                fs[pl.ds(at, 16), col : col + 128] = out[i][16 * e : 16 * e + 16].astype(BF16)

    def edge_step(j, carry):
        for copy in halo(j):
            copy.wait_recv()
        for u in (-1, 0, 1):
            edge(CHUNK * j + u)
        return carry

    for copy in halo(0):
        copy.wait_recv()
    edge(0)
    edge(1)
    lax.fori_loop(1, CHUNKS, edge_step, 0)
    edge(GROUPS - 1)

    f_copy = pltpu.make_async_copy(fs, f_hbm, f_sem)
    f_copy.start()

    for k in (0, 14):
        left, right = outer(k * COLS, (k + 2) * COLS)
        gs[:, 0:256] += left
        gs[256:BP, 256:BP] += right

    for t, (rt, ct) in enumerate(LOWER):
        pk[t] = gs[8 * rt : 8 * rt + 8, 128 * ct : 128 * ct + 128]
    for t in range(len(LOWER), 128):
        pk[t] = jnp.zeros((8, 128), F32)

    mine, other = pl.ds(64 * core, 64), pl.ds(64 * (1 - core), 64)
    pair = pltpu.make_async_remote_copy(
        src_ref=pk.at[other], dst_ref=r1, send_sem=ex_send.at[0], recv_sem=ex_recv.at[0],
        device_id=sibling, device_id_type=MESH,
    )
    pair.start()
    pair.wait_recv()
    pk[mine] += r1[...]

    def scatter(d, carry):
        to, device = peer(d)
        pltpu.make_async_remote_copy(
            src_ref=pk.at[64 * core + to], dst_ref=r2.at[d - 1], send_sem=ex_send.at[1], recv_sem=ex_recv.at[1],
            device_id=device, device_id_type=MESH,
        ).start()
        return carry

    lax.fori_loop(1, 64, scatter, 0)
    pltpu.make_async_copy(r2, r2, ex_recv.at[1]).wait()
    ag[64 * core + chip] = pk[64 * core + chip] + jnp.sum(r2[...], axis=0)

    def gather(d, carry):
        device = peer(d)[1]
        tile = ag.at[64 * core + chip]
        pltpu.make_async_remote_copy(
            src_ref=tile, dst_ref=tile, send_sem=ex_send.at[2], recv_sem=ex_recv.at[2],
            device_id=device, device_id_type=MESH,
        ).start()
        return carry

    lax.fori_loop(1, 64, gather, 0)
    pltpu.make_async_copy(r2, r2, ex_recv.at[2]).wait()
    swap = pltpu.make_async_remote_copy(
        src_ref=ag.at[mine], dst_ref=ag.at[mine], send_sem=ex_send.at[3], recv_sem=ex_recv.at[3],
        device_id=sibling, device_id_type=MESH,
    )
    swap.start()
    swap.wait_recv()
    g_ref[...] = ag[...]

    swap.wait_send()
    pair.wait_send()
    pltpu.make_async_copy(r2, r2, ex_send.at[1]).wait()
    pltpu.make_async_copy(r2, r2, ex_send.at[2]).wait()

    def sent(j, carry):
        for copy in halo(j):
            copy.wait_send()
        return carry

    lax.fori_loop(0, CHUNKS, sent, 0)
    f_copy.wait()


def split3(a):
    hi = a.astype(BF16)
    rest = a - hi.astype(F32)
    mid = rest.astype(BF16)
    low = (rest - mid.astype(F32)).astype(BF16)
    return hi, mid, low


def dot6(a, b, dims):
    n = a.shape[0]
    parts = jnp.concatenate(split3(a), axis=0)
    one = lax.dot_general(parts, b[0], dims, preferred_element_type=F32)
    two = lax.dot_general(parts[: 2 * n], b[1], dims, preferred_element_type=F32)
    three = lax.dot_general(parts[:n], b[2], dims, preferred_element_type=F32)
    return one[:n] + (((one[2 * n :] + two[n:]) + three) + (one[n : 2 * n] + two[:n]))


NN = (((1,), (0,)), ((), ()))


def inverse_factor(s):
    ri, ci = iotas((8, 128))
    blocks = [s[8 * i : 8 * i + 8] + (ci == ri + 64 + 8 * i).astype(F32) for i in range(8)]
    for j in range(RANK):
        pb, pr = divmod(j, 8)
        col = blocks[pb][:, j : j + 1]
        scaled = (blocks[pb] * (1.0 / col))[pr : pr + 1]
        for i in range(pb, 8):
            c = blocks[i][:, j : j + 1]
            if i == pb:
                if pr == 7:
                    continue
                c = jnp.where(ri[:, 0:1] > pr, c, 0.0)
            blocks[i] = blocks[i] - c * scaled
    out = []
    for i in range(8):
        diag = jnp.sum(jnp.where(ci == ri + 8 * i, blocks[i], 0.0), axis=1, keepdims=True)
        out.append(blocks[i] * lax.rsqrt(diag))
    return jnp.concatenate(out, axis=0)


def iterate_kernel(g_ref, start_ref, f_hbm, proj_ref, scores_hbm, gf, gh, gm, gl, tt, fs, sc, f_sem, o_sem):
    f_copy = pltpu.make_async_copy(f_hbm, fs, f_sem)
    f_copy.start()

    gf[BP:512, :] = jnp.zeros((512 - BP, 512), F32)
    for t, (rt, ct) in enumerate(LOWER):
        tile = g_ref[t]
        if rt == 53 or ct == 3:
            ri, ci = iotas((8, 128))
            tile = jnp.where((ri + 8 * rt < BANDS) & (ci + 128 * ct < BANDS), tile, 0.0)
        gf[8 * rt : 8 * rt + 8, 128 * ct : 128 * ct + 128] = tile
    for i in range(4):
        for j in range(i):
            gf[128 * j : 128 * j + 128, 128 * i : 128 * i + 128] = gf[
                128 * i : 128 * i + 128, 128 * j : 128 * j + 128
            ].T
    for ref, part in zip((gh, gm, gl), split3(gf[...])):
        ref[...] = part

    tt[:, 384:512] = jnp.zeros((RANK, 128), F32)
    tt[:, 0:BANDS] = start_ref[...].T

    zeros = jnp.zeros((RANK, 512), BF16)

    def normaliser(t):
        h, m, l = split3(t)
        rhs = tuple(jnp.concatenate([p, zeros], axis=0) for p in (h, m, l))
        return inverse_factor(dot6(t, rhs, NT))

    def apply(w, t):
        rhs = tuple(jnp.concatenate([zeros, p], axis=0) for p in split3(t))
        return dot6(w, rhs, NN)

    def step(i, carry):
        t = tt[...]
        z = dot6(t, (gh[...], gm[...], gl[...]), NN)
        tt[...] = apply(normaliser(t), z)
        return carry

    lax.fori_loop(0, ITERS, step, 0)
    t = tt[...]
    basis = apply(normaliser(t), t)

    h, m, l = split3(basis)
    lhs = jnp.concatenate([h, h, m, m], axis=0).astype(F32).T.astype(BF16)
    rhs = jnp.concatenate([h, m, h, m], axis=0)
    proj = jnp.dot(lhs, rhs, preferred_element_type=F32)
    proj_ref[...] = proj[0:BANDS, 0:BANDS]

    f_copy.wait()
    narrow = h[:, 0:BP]

    def score(r, carry):
        cols = pl.ds(pl.multiple_of(r * COLS, 128), COLS)
        s = jnp.dot(narrow, fs[:, cols], preferred_element_type=F32)
        for i in range(3):
            sc[pl.ds(RANK * ROWS * i + r, RANK, stride=ROWS), :] = s[:, 128 * i : 128 * i + 128]
        return carry

    lax.fori_loop(0, ROWS, score, 0)
    out = [
        pltpu.make_async_copy(
            sc.at[pl.ds(RANK * ROWS * i, RANK * ROWS)], scores_hbm.at[:, pl.ds(128 * i, 128)], o_sem.at[i]
        )
        for i in range(3)
    ]
    for copy in out:
        copy.start()
    for copy in out:
        copy.wait()


def on_device(radiance, counts, start):
    x = radiance.reshape(BANDS * ROWS, COLS)
    vmem = pl.BlockSpec(memory_space=pltpu.VMEM)
    anym = pl.BlockSpec(memory_space=pl.ANY)
    dma = pltpu.SemaphoreType.DMA
    features, tiles = pl.pallas_call(
        features_kernel,
        out_shape=(
            jax.ShapeDtypeStruct((BP, ROWS * COLS), BF16),
            jax.ShapeDtypeStruct((128, 8, 128), F32),
        ),
        in_specs=[pl.BlockSpec(memory_space=pltpu.SMEM), anym],
        out_specs=(anym, vmem),
        scratch_shapes=[
            pltpu.VMEM((ROWS * (BP + 2), COLS), BF16),
            pltpu.VMEM((HR, COLS), BF16),
            pltpu.VMEM((HR, COLS), BF16),
            pltpu.VMEM((HR, COLS), BF16),
            pltpu.VMEM((HR, COLS), BF16),
            pltpu.VMEM((BP, ROWS * COLS), BF16),
            pltpu.VMEM((4, BP, COLS), F32),
            pltpu.VMEM((BP, 512), F32),
            pltpu.VMEM((128, 8, 128), F32),
            pltpu.VMEM((64, 8, 128), F32),
            pltpu.VMEM((63, 8, 128), F32),
            pltpu.VMEM((128, 8, 128), F32),
            dma((CHUNKS,)),
            dma,
            dma((CHUNKS,)),
            dma((CHUNKS,)),
            dma((CHUNKS,)),
            dma((CHUNKS,)),
            dma((4,)),
            dma((4,)),
        ],
        compiler_params=pltpu.CompilerParams(
            collective_id=0, has_side_effects=True, vmem_limit_bytes=48 * 2**20
        ),
    )(counts, x)
    projector, scores = pl.pallas_call(
        iterate_kernel,
        out_shape=(
            jax.ShapeDtypeStruct((BANDS, BANDS), F32),
            jax.ShapeDtypeStruct((RANK * ROWS, COLS), F32),
        ),
        in_specs=[vmem, vmem, anym],
        out_specs=(vmem, anym),
        scratch_shapes=[
            pltpu.VMEM((512, 512), F32),
            pltpu.VMEM((512, 512), BF16),
            pltpu.VMEM((512, 512), BF16),
            pltpu.VMEM((512, 512), BF16),
            pltpu.VMEM((RANK, 512), F32),
            pltpu.VMEM((BP, ROWS * COLS), BF16),
            pltpu.VMEM((3 * RANK * ROWS, 128), F32),
            dma,
            dma((3,)),
        ],
        compiler_params=pltpu.CompilerParams(vmem_limit_bytes=48 * 2**20),
    )(tiles, start, features)
    return projector, scores.reshape(1, RANK, ROWS, COLS)


def solution(mesh):
    return jax.shard_map(
        on_device,
        mesh=mesh,
        in_specs=(P("line", None, "track", None), P("line", "track"), P()),
        out_specs=(P(), P("line", None, "track", None)),
        check_vma=False,
    )
```

time: 1120 us -> 111 us (0.10); the launches traced: 1110 us -> 111 us
  waiting for transfers between devices: 830 us -> 0 us
  other arithmetic: 155 us -> 0 us
  Pallas kernels: 0 us -> 104 us
  matrix products: 84.3 us -> 0 us
  between operations: 15.8 us -> 1.31 us
    psum x6 -> x0, waiting for transfers between devices: 826 us -> none  [on_device(): summed = lax.psum(image, ('line', 'track'))]
    pallas_call x0 -> x2, Pallas kernels: none -> 104 us  [the longest x1 55.5 us: on_device(): pl.pallas_call(features_kernel, out_shape=(jax.ShapeDtypeStruct((BP, ROWS...]
    another operation x35 -> x0, other arithmetic: 84.6 us -> none  [the longest x21 45.6 us: orthonormal(): factor = jnp.linalg.cholesky(inner)]
    dot_general x21 -> x0, matrix products: 76.4 us -> none  [the longest x6 34.6 us: on_device(): jnp.dot(features, coords.T, precision=lax.Precision.HIGHEST, preferred_el...]
    div x9 -> x0, other arithmetic: 50.1 us -> none  [the longest x1 25.5 us: make_features(): (padded[:, 0:rows_out] + 4.0 * padded[:, 1:rows_out + 1] + 6.0 * padded[:...]
    convert_element_type x3 -> x0, other arithmetic: 16.3 us -> none  [the longest x1 8.55 us: make_features(): return derived.astype(jnp.bfloat16).reshape(derived.shape[0], -1)]
  transfers between devices with their start and end apart: 8 -> 0, of which waited for: 7 -> 0; matrix products, arithmetic and copies ran while one was open for 2% -> 0% of each run, Pallas kernels for 0% -> 0%
where the time goes in v1:
time: 111 us
  Pallas kernels  104 us (94%)
  local copies, waits for them, and re-layouts  6 us (5%)
  between operations  1.31 us (1%)
    pallas_call x1, Pallas kernels, on_device(): pl.pallas_call(features_kernel, out_shape=(jax.ShapeDtypeStruct((BP, ROWS...  55.5 us
    pallas_call x1, Pallas kernels, on_device(): pl.pallas_call(iterate_kernel, out_shape=(jax.ShapeDtypeStruct((BANDS, BA...  48.5 us
    unnamed x5, local copies, waits for them, and re-layouts  6 us

profile of v1, /device:TPU:1, one launch (start us, length us, event | category | flops | bytes accessed | tf_op | source)
XLA Modules:
  0.0 111.3 jit_solution(3171952233369111013)
XLA Ops:
  1.3 1.0 copy.5.start_ref
  2.3 0.0 copy-start.1
  2.3 2.5 %copy-done.1 = bf16[1,425,16,384]{3,2,1,0:T(8,128)(2,1)S(1)} copy-done((bf16[1,425,16,384]{3,2,1,0:T(8,128)(2,1)S(1)}, bf16[1,425,16,384]{3,2,1,0:T(8,128)(2,1)}, u32[]{:S(2)}) %copy-start.1) | copy-done | bytes 5222424
  4.8 55.5 %shard_map.50 = (bf16[432,6144]{1,0:T(8,128)(2,1)}, f32[128,8,128]{2,1,0:T(8,128)S(1)}) custom-call(s32[1,1]{1,0:T(1,128)S(6)} %copy.6.counts_ref, bf16[6800,384]{1,0:T(8,128)(2,1)S(1)} %bitcast.2), custom_call_target="tpu_custom_call" | custom-call | tf_op jit(solution)/shard_map/pallas_call | solution.py:391
  60.3 0.0 copy-start
  60.3 2.5 %copy-done = bf16[432,6144]{1,0:T(8,128)(2,1)S(1)} copy-done((bf16[432,6144]{1,0:T(8,128)(2,1)S(1)}, bf16[432,6144]{1,0:T(8,128)(2,1)}, u32[]{:S(2)}) %copy-start) | copy-done | bytes 5308440
  62.8 48.5 %shard_map.51 = (f32[425,425]{1,0:T(8,128)}, f32[1024,384]{1,0:T(8,128)}) custom-call(f32[128,8,128]{2,1,0:T(8,128)S(1)} %get-tuple-element.6.g_ref, f32[425,64]{1,0:T(8,128)S(1)} %copy.5.start_ref, bf16[432,6144]{1,0:T(8,128)(2,1)S(1)} %copy-done), custom_call_target="tpu_custom_call" | custom-call | tf_op jit(solution)/shard_map/pallas_call | solution.py:425
Async XLA Ops:
  2.3 2.5 %copy-start.1 = (bf16[1,425,16,384]{3,2,1,0:T(8,128)(2,1)S(1)}, bf16[1,425,16,384]{3,2,1,0:T(8,128)(2,1)}, u32[]{:S(2)}) copy-start(bf16[1,425,16,384]{3,2,1,0:T(8,128)(2,1)} %param.3) | copy-start | bytes 15667204
  60.3 2.5 %copy-start = (bf16[432,6144]{1,0:T(8,128)(2,1)S(1)}, bf16[432,6144]{1,0:T(8,128)(2,1)}, u32[]{:S(2)}) copy-start(bf16[432,6144]{1,0:T(8,128)(2,1)} %get-tuple-element.7.f_hbm) | copy-start | bytes 15925252

commit v2 on v1

--- a/solution.py
+++ b/solution.py
@@ -290,25 +290,35 @@
 NN = (((1,), (0,)), ((), ()))
 
 
+def reciprocal(d):
+    return 1.0 / d
+
+
 def inverse_factor(s):
     ri, ci = iotas((8, 128))
-    blocks = [s[8 * i : 8 * i + 8] + (ci == ri + 64 + 8 * i).astype(F32) for i in range(8)]
-    for j in range(RANK):
-        pb, pr = divmod(j, 8)
-        col = blocks[pb][:, j : j + 1]
-        scaled = (blocks[pb] * (1.0 / col))[pr : pr + 1]
-        for i in range(pb, 8):
-            c = blocks[i][:, j : j + 1]
-            if i == pb:
-                if pr == 7:
+    rows = [s[8 * i : 8 * i + 8] + (ci == ri + 64 + 8 * i).astype(F32) for i in range(8)]
+    spread = lambda v, k: jnp.broadcast_to(v[k : k + 1], (8, 128))
+    for p in range(8):
+        cols = {
+            i: [jnp.broadcast_to(rows[i][:, 8 * p + l : 8 * p + l + 1], (8, 128)) for l in range(8)]
+            for i in range(p, 8)
+        }
+        pivots = jnp.ones((8, 128), F32)
+        for k in range(8):
+            pivot = spread(cols[p][k], k)
+            pivots = jnp.where(ri == k, pivot, pivots)
+            inv = reciprocal(pivot)
+            heads = [spread(cols[p][l], k) * inv for l in range(k + 1, 8)]
+            row = spread(rows[p], k) * inv
+            for i in range(p, 8):
+                if i == p and k == 7:
                     continue
-                c = jnp.where(ri[:, 0:1] > pr, c, 0.0)
-            blocks[i] = blocks[i] - c * scaled
-    out = []
-    for i in range(8):
-        diag = jnp.sum(jnp.where(ci == ri + 8 * i, blocks[i], 0.0), axis=1, keepdims=True)
-        out.append(blocks[i] * lax.rsqrt(diag))
-    return jnp.concatenate(out, axis=0)
+                m = jnp.where(ri > k, cols[i][k], 0.0) if i == p else cols[i][k]
+                for l in range(k + 1, 8):
+                    cols[i][l] = cols[i][l] - m * heads[l - k - 1]
+                rows[i] = rows[i] - m * row
+        rows[p] = rows[p] * lax.rsqrt(pivots)
+    return jnp.concatenate(rows, axis=0)
 
 
 def iterate_kernel(g_ref, start_ref, f_hbm, proj_ref, scores_hbm, gf, gh, gm, gl, tt, fs, sc, f_sem, o_sem):
@@ -331,7 +341,7 @@
         ref[...] = part
 
     tt[:, 384:512] = jnp.zeros((RANK, 128), F32)
-    tt[:, 0:BANDS] = start_ref[...].T
+    tt[:, 0:BANDS] = start_ref[...]
 
     zeros = jnp.zeros((RANK, 512), BF16)
 
@@ -383,10 +393,37 @@
         copy.wait()
 
 
+def second(tiles, start, features):
+    vmem = pl.BlockSpec(memory_space=pltpu.VMEM)
+    hbm = pl.BlockSpec(memory_space=pltpu.HBM)
+    dma = pltpu.SemaphoreType.DMA
+    return pl.pallas_call(
+        iterate_kernel,
+        out_shape=(
+            jax.ShapeDtypeStruct((BANDS, BANDS), F32),
+            jax.ShapeDtypeStruct((RANK * ROWS, COLS), F32),
+        ),
+        in_specs=[vmem, vmem, hbm],
+        out_specs=(vmem, hbm),
+        scratch_shapes=[
+            pltpu.VMEM((512, 512), F32),
+            pltpu.VMEM((512, 512), BF16),
+            pltpu.VMEM((512, 512), BF16),
+            pltpu.VMEM((512, 512), BF16),
+            pltpu.VMEM((RANK, 512), F32),
+            pltpu.VMEM((BP, ROWS * COLS), BF16),
+            pltpu.VMEM((3 * RANK * ROWS, 128), F32),
+            dma,
+            dma((3,)),
+        ],
+        compiler_params=pltpu.CompilerParams(vmem_limit_bytes=56 * 2**20),
+    )(tiles, start.T, features)
+
+
 def on_device(radiance, counts, start):
     x = radiance.reshape(BANDS * ROWS, COLS)
     vmem = pl.BlockSpec(memory_space=pltpu.VMEM)
-    anym = pl.BlockSpec(memory_space=pl.ANY)
+    hbm = pl.BlockSpec(memory_space=pltpu.HBM)
     dma = pltpu.SemaphoreType.DMA
     features, tiles = pl.pallas_call(
         features_kernel,
@@ -394,8 +431,8 @@
             jax.ShapeDtypeStruct((BP, ROWS * COLS), BF16),
             jax.ShapeDtypeStruct((128, 8, 128), F32),
         ),
-        in_specs=[pl.BlockSpec(memory_space=pltpu.SMEM), anym],
-        out_specs=(anym, vmem),
+        in_specs=[pl.BlockSpec(memory_space=pltpu.SMEM), hbm],
+        out_specs=(hbm, vmem),
         scratch_shapes=[
             pltpu.VMEM((ROWS * (BP + 2), COLS), BF16),
             pltpu.VMEM((HR, COLS), BF16),
@@ -419,30 +456,10 @@
             dma((4,)),
         ],
         compiler_params=pltpu.CompilerParams(
-            collective_id=0, has_side_effects=True, vmem_limit_bytes=48 * 2**20
+            collective_id=0, has_side_effects=True, vmem_limit_bytes=56 * 2**20
         ),
     )(counts, x)
-    projector, scores = pl.pallas_call(
-        iterate_kernel,
-        out_shape=(
-            jax.ShapeDtypeStruct((BANDS, BANDS), F32),
-            jax.ShapeDtypeStruct((RANK * ROWS, COLS), F32),
-        ),
-        in_specs=[vmem, vmem, anym],
-        out_specs=(vmem, anym),
-        scratch_shapes=[
-            pltpu.VMEM((512, 512), F32),
-            pltpu.VMEM((512, 512), BF16),
-            pltpu.VMEM((512, 512), BF16),
-            pltpu.VMEM((512, 512), BF16),
-            pltpu.VMEM((RANK, 512), F32),
-            pltpu.VMEM((BP, ROWS * COLS), BF16),
-            pltpu.VMEM((3 * RANK * ROWS, 128), F32),
-            dma,
-            dma((3,)),
-        ],
-        compiler_params=pltpu.CompilerParams(vmem_limit_bytes=48 * 2**20),
-    )(tiles, start, features)
+    projector, scores = second(tiles, start, features)
     return projector, scores.reshape(1, RANK, ROWS, COLS)
 
 

time: 111 us -> 80.7 us (0.73)
  Pallas kernels: 104 us -> 79.3 us
  local copies, waits for them, and re-layouts: 6 us -> 0 us
    pallas_call x1, Pallas kernels: 48.5 us -> 24.1 us  [second(): pl.pallas_call(iterate_kernel, out_shape=(jax.ShapeDtypeStruct((BANDS, BA...]
    unnamed x5 -> x0, local copies, waits for them, and re-layouts: 6 us -> none
where the time goes in v2:
time: 80.7 us; the launch traced here: 80.6 us
  Pallas kernels  79.3 us (98%)
  between operations  1.28 us (2%)
    pallas_call x1, Pallas kernels, on_device(): pl.pallas_call(features_kernel, out_shape=(jax.ShapeDtypeStruct((BP, ROWS...  55.1 us
    pallas_call x1, Pallas kernels, second(): pl.pallas_call(iterate_kernel, out_shape=(jax.ShapeDtypeStruct((BANDS, BA...  24.1 us

profile of v2, /device:TPU:1, one launch (start us, length us, event | category | flops | bytes accessed | tf_op | source)
XLA Modules:
  0.0 80.6 jit_solution(13675370026170938366)
XLA Ops:
  1.3 55.1 %shard_map.50 = (bf16[432,6144]{1,0:T(8,128)(2,1)}, f32[128,8,128]{2,1,0:T(8,128)}) custom-call(s32[1,1]{1,0:T(1,128)S(6)} %copy.5.counts_ref, bf16[6800,384]{1,0:T(8,128)(2,1)} %bitcast.3), custom_call_target="tpu_custom_call" | custom-call | tf_op jit(solution)/shard_map/pallas_call | solution.py:428
  56.4 24.1 %shard_map.51 = (f32[425,425]{1,0:T(8,128)}, f32[1024,384]{1,0:T(8,128)}) custom-call(f32[128,8,128]{2,1,0:T(8,128)} %get-tuple-element.6.g_ref, f32[64,425]{1,0:T(8,128)} %bitcast.4, bf16[432,6144]{1,0:T(8,128)(2,1)} %get-tuple-element.7.f_hbm), custom_call_target="tpu_custom_call" | custom-call | tf_op jit(solution)/shard_map/pallas_call | solution.py:400

commit v3 on v2

--- a/solution.py
+++ b/solution.py
@@ -32,41 +32,50 @@
     return lax.broadcasted_iota(jnp.int32, shape, 0), lax.broadcasted_iota(jnp.int32, shape, 1)
 
 
-def smooth_cols(t):
-    rows = t.shape[0]
-    lane = lax.broadcasted_iota(jnp.int32, (rows, 128), 1)
-    first, last = lane == 0, lane == 127
-    x = [t[:, 128 * i : 128 * i + 128] for i in range(3)]
-
-    def right(v, edge):
-        r = [pltpu.roll(a, 1, 1) for a in v]
-        return [jnp.where(first, p, a) for p, a in zip([edge] + r[:2], r)]
-
-    def left(v, edge):
-        r = [pltpu.roll(a, 127, 1) for a in v]
-        return [jnp.where(last, n, a) for n, a in zip(r[1:] + [edge], r)]
-
-    zero = jnp.zeros((rows, 128), F32)
-    v = [a + b for a, b in zip(x, right(x, zero))]
-    y = [a + b for a, b in zip(v, left(v, x[2]))]
-    w = [a + b for a, b in zip(y, right(y, x[0]))]
-    return [a + b for a, b in zip(w, left(w, x[2] + y[2]))]
+def banded(rows, cols, shift):
+    ri, ci = iotas((rows, cols))
+    return BIN(jnp.abs(ri + shift - ci)).astype(BF16)
+
+
+def split2(t, hi_ref, lo_ref, rows):
+    hi = t.astype(BF16)
+    hi_ref[rows, :] = hi
+    lo_ref[rows, :] = (t - hi.astype(F32)).astype(BF16)
+
+
+def smooth_cols(hi_ref, lo_ref, wl_ref, wr_ref, rows):
+    hi, lo = hi_ref[0:rows, :], lo_ref[0:rows, :]
+    left = jnp.concatenate([hi[:, 0:256], lo[:, 0:256], hi[:, 256:384], lo[:, 256:384]], axis=1)
+    right = jnp.concatenate([hi[:, 128:384], lo[:, 128:384]], axis=1)
+    return (
+        jnp.dot(left, wl_ref[...], preferred_element_type=F32),
+        jnp.dot(right, wr_ref[...], preferred_element_type=F32),
+    )
 
 
 def features_kernel(
     counts_ref, x_hbm, f_hbm, g_ref,
-    xs, su, sd, hu, hd, fs, tb, gs, pk, r1, r2, ag,
-    x_sem, f_sem, su_sem, sd_sem, hu_sem, hd_sem, ex_send, ex_recv,
+    xs, su, sd, hu, hd, fs, th, tl, wl, wr, tb, gs, pk, r1, r2, ag,
+    x_sem, f_sem, su_sem, sd_sem, hu_sem, hd_sem, ex_send, ex_recv, line_sem,
 ):
     line, track = lax.axis_index("line"), lax.axis_index("track")
     y, core = line // 2, line % 2
     xx, z = track // 4, track % 4
-    chip = 16 * xx + 4 * y + z
     sibling = (2 * y + 1 - core, track)
 
-    def peer(d):
-        px, py, pz = (xx + d // 16) % 4, (y + (d // 4) % 4) % 4, (z + d % 4) % 4
+    here = (xx, y, z)
+    near = [[lax.rem(base + step, 4) for step in range(4)] for base in here]
+
+    def peer(*steps):
+        px, py, pz = (near[i][steps[i]] for i in range(3))
         return 16 * px + 4 * py + pz, (2 * py + core, 4 * px + pz)
+
+    on_axis = [[peer(*[step if i == axis else 0 for i in range(3)])[1] for step in (1, 2, 3)] for axis in range(3)]
+    others = [(i, j, k) for i in range(4) for j in range(4) for k in range(4)][1:]
+    others.sort(key=lambda steps: -sum(min(v, 4 - v) for v in steps))
+
+    before, after = (line, lax.rem(track + TILES - 1, TILES)), (line, lax.rem(track + 1, TILES))
+    greeted = [sibling, before, after] + on_axis[0] + on_axis[1] + on_axis[2]
 
     crow = 256 * CHUNK
 
@@ -80,13 +89,8 @@
         load(j).start()
 
     barrier = pltpu.get_barrier_semaphore()
-    pl.semaphore_signal(barrier, inc=1, device_id=sibling, device_id_type=MESH)
-
-    def greet(d, carry):
-        pl.semaphore_signal(barrier, inc=1, device_id=peer(d)[1], device_id_type=MESH)
-        return carry
-
-    lax.fori_loop(1, 64, greet, 0)
+    for device in greeted:
+        pl.semaphore_signal(barrier, inc=1, device_id=device, device_id_type=MESH)
 
     xs[0:16, :] = jnp.zeros((16, COLS), BF16)
     tail = ROWS * (BANDS + 1)
@@ -94,12 +98,36 @@
     for h in (hu, hd):
         h[0:16, :] = jnp.zeros((16, COLS), BF16)
         h[HR - 16 : HR, :] = jnp.zeros((16, COLS), BF16)
-    gs[:, 384:512] = jnp.zeros((BP, 128), F32)
 
     cnt = counts_ref[0, 0]
     ri, ci = iotas((64, 256))
     want = jnp.where(ri < 32, ri & 1, 14 + (ri & 1))
     sel = ((((ri & 31) >> 1) == (ci >> 4)) & (want == (ci & 15)) & (want < cnt)).astype(F32).astype(BF16)
+
+    def halo(j):
+        rows = pl.ds(pl.multiple_of(16 + 32 * CHUNK * j, 32 * CHUNK // 6), 32 * CHUNK)
+        first = pltpu.make_async_remote_copy(
+            src_ref=su.at[rows], dst_ref=hd.at[rows], send_sem=su_sem.at[j], recv_sem=hd_sem.at[j],
+            device_id=before, device_id_type=MESH,
+        )
+        last = pltpu.make_async_remote_copy(
+            src_ref=sd.at[rows], dst_ref=hu.at[rows], send_sem=sd_sem.at[j], recv_sem=hu_sem.at[j],
+            device_id=after, device_id_type=MESH,
+        )
+        return first, last
+
+    for j in range(CHUNKS):
+        load(j).wait()
+        for g in range(CHUNK * j, CHUNK * j + CHUNK):
+            picked = jnp.dot(sel, xs[16 + 256 * g : 272 + 256 * g, :], preferred_element_type=F32).astype(BF16)
+            su[16 + 32 * g : 48 + 32 * g, :] = picked[0:32]
+            sd[16 + 32 * g : 48 + 32 * g, :] = picked[32:64]
+        if j == 0:
+            pl.semaphore_wait(barrier, len(greeted))
+            for device in on_axis[1]:
+                pl.semaphore_signal(line_sem.at[0], inc=1, device_id=device, device_id_type=MESH)
+        for copy in halo(j):
+            copy.start()
 
     ri, ci = iotas((128, 160))
     r, b, bi, rr = ri >> 3, ri & 7, ci >> 4, ci & 15
@@ -118,51 +146,38 @@
     wt = jnp.where((r < cnt) & have, BIN(jnp.abs(rr - r)), 0.0)
     rim = (sign * wt * (1.0 / 512.0)).astype(BF16)
 
-    def halo(j):
-        rows = pl.ds(pl.multiple_of(16 + 32 * CHUNK * j, 32 * CHUNK // 6), 32 * CHUNK)
-        first = pltpu.make_async_remote_copy(
-            src_ref=su.at[rows], dst_ref=hd.at[rows], send_sem=su_sem.at[j], recv_sem=hd_sem.at[j],
-            device_id=(line, (track + TILES - 1) % TILES), device_id_type=MESH,
-        )
-        last = pltpu.make_async_remote_copy(
-            src_ref=sd.at[rows], dst_ref=hu.at[rows], send_sem=sd_sem.at[j], recv_sem=hu_sem.at[j],
-            device_id=(line, (track + 1) % TILES), device_id_type=MESH,
-        )
-        return first, last
-
-    for j in range(CHUNKS):
-        load(j).wait()
-        for g in range(CHUNK * j, CHUNK * j + CHUNK):
-            picked = jnp.dot(sel, xs[16 + 256 * g : 272 + 256 * g, :], preferred_element_type=F32).astype(BF16)
-            su[16 + 32 * g : 48 + 32 * g, :] = picked[0:32]
-            sd[16 + 32 * g : 48 + 32 * g, :] = picked[32:64]
-        if j == 0:
-            pl.semaphore_wait(barrier, 64)
-        for copy in halo(j):
-            copy.start()
-
-    def interior(g):
-        at = pl.multiple_of(16 * g, 16)
-        halves = []
-        for h in range(2):
-            xk = xs[pl.ds(pl.multiple_of(256 * g + 128 * h, 128), 160), :]
+    wl[0:256, :] = banded(256, 256, 0)
+    wl[256:512, :] = banded(256, 256, 0)
+    wl[512:640, :] = banded(128, 256, 256)
+    wl[640:768, :] = banded(128, 256, 256)
+    wr[0:256, :] = banded(256, 128, -128)
+    wr[256:512, :] = banded(256, 128, -128)
+
+    gs[:, 384:512] = jnp.zeros((BP, 128), F32)
+
+    def interior_step(s, carry):
+        for u in range(2 * CHUNK):
+            at = pl.multiple_of(16 * CHUNK * s + 8 * u, 8)
+            xk = xs[pl.ds(pl.multiple_of(256 * CHUNK * s + 128 * u, 128), 160), :]
             t = jnp.dot(body, xk, preferred_element_type=F32)
             for e, row in enumerate(EDGE):
-                tb[e, pl.ds(pl.multiple_of(at + 8 * h, 8), 8), :] = t[8 * row : 8 * row + 8]
-            halves.append(smooth_cols(t[16:112]))
-        for row in range(2, 14):
-            k = 8 * (row - 2)
-            for i in range(3):
-                both = jnp.concatenate([halves[0][i][k : k + 8], halves[1][i][k : k + 8]], axis=0)
-                col = row * COLS + 128 * i
-                fs[pl.ds(at, 16), col : col + 128] = both.astype(BF16)
-
-    def interior_step(s, carry):
-        for u in range(3):
-            interior(3 * s + u)
+                tb[e, pl.ds(at, 8), :] = t[8 * row : 8 * row + 8]
+            split2(t[16:112], th, tl, slice(96 * u, 96 * u + 96))
+        wide = smooth_cols(th, tl, wl, wr, 192 * CHUNK)
+        for u in range(CHUNK):
+            at = pl.ds(pl.multiple_of(16 * CHUNK * s + 16 * u, 16), 16)
+            for row in range(2, 14):
+                k = 192 * u + 8 * (row - 2)
+                for part, col in zip(wide, (row * COLS, row * COLS + 256)):
+                    both = jnp.concatenate([part[k : k + 8], part[k + 96 : k + 104]], axis=0)
+                    fs[at, col : col + part.shape[1]] = both.astype(BF16)
         return carry
 
-    lax.fori_loop(0, GROUPS // 3, interior_step, 0)
+    lax.fori_loop(0, CHUNKS, interior_step, 0)
+
+    pl.semaphore_wait(line_sem.at[0], 3)
+    for device in on_axis[2]:
+        pl.semaphore_signal(line_sem.at[1], inc=1, device_id=device, device_id_type=MESH)
 
     def outer(lo, hi):
         a = fs[:, lo:hi]
@@ -178,30 +193,32 @@
         gs[:, 0:256] += left
         gs[256:BP, 256:BP] += right
 
-    def edge(g):
-        at = pl.multiple_of(16 * g, 16)
-        src = pl.ds(pl.multiple_of(32 * g, 32), 64)
-        halos = jnp.concatenate([hu[src, :], hd[src, :]], axis=0)
-        t = jnp.dot(rim, halos, preferred_element_type=F32) + tb[:, pl.ds(at, 16), :].reshape(64, COLS)
-        out = smooth_cols(t)
-        for e, row in enumerate(EDGE):
-            for i in range(3):
-                col = row * COLS + 128 * i
-                fs[pl.ds(at, 16), col : col + 128] = out[i][16 * e : 16 * e + 16].astype(BF16)
+    def edges(first, count):
+        for u in range(count):
+            at = pl.multiple_of(16 * (first + u), 16)
+            src = pl.ds(pl.multiple_of(32 * (first + u), 32), 64)
+            halos = jnp.concatenate([hu[src, :], hd[src, :]], axis=0)
+            t = jnp.dot(rim, halos, preferred_element_type=F32) + tb[:, pl.ds(at, 16), :].reshape(64, COLS)
+            split2(t, th, tl, slice(64 * u, 64 * u + 64))
+        wide = smooth_cols(th, tl, wl, wr, 64 * count)
+        for u in range(count):
+            at = pl.ds(pl.multiple_of(16 * (first + u), 16), 16)
+            for e, row in enumerate(EDGE):
+                k = 64 * u + 16 * e
+                for part, col in zip(wide, (row * COLS, row * COLS + 256)):
+                    fs[at, col : col + part.shape[1]] = part[k : k + 16].astype(BF16)
 
     def edge_step(j, carry):
         for copy in halo(j):
             copy.wait_recv()
-        for u in (-1, 0, 1):
-            edge(CHUNK * j + u)
+        edges(CHUNK * j - 1, CHUNK)
         return carry
 
     for copy in halo(0):
         copy.wait_recv()
-    edge(0)
-    edge(1)
+    edges(0, CHUNK - 1)
     lax.fori_loop(1, CHUNKS, edge_step, 0)
-    edge(GROUPS - 1)
+    edges(GROUPS - 1, 1)
 
     f_copy = pltpu.make_async_copy(fs, f_hbm, f_sem)
     f_copy.start()
@@ -216,50 +233,35 @@
     for t in range(len(LOWER), 128):
         pk[t] = jnp.zeros((8, 128), F32)
 
-    mine, other = pl.ds(64 * core, 64), pl.ds(64 * (1 - core), 64)
-    pair = pltpu.make_async_remote_copy(
-        src_ref=pk.at[other], dst_ref=r1, send_sem=ex_send.at[0], recv_sem=ex_recv.at[0],
-        device_id=sibling, device_id_type=MESH,
-    )
-    pair.start()
-    pair.wait_recv()
-    pk[mine] += r1[...]
-
-    def scatter(d, carry):
-        to, device = peer(d)
+    def send(phase, src, dst, device):
         pltpu.make_async_remote_copy(
-            src_ref=pk.at[64 * core + to], dst_ref=r2.at[d - 1], send_sem=ex_send.at[1], recv_sem=ex_recv.at[1],
+            src_ref=src, dst_ref=dst, send_sem=ex_send.at[phase], recv_sem=ex_recv.at[phase],
             device_id=device, device_id_type=MESH,
         ).start()
-        return carry
-
-    lax.fori_loop(1, 64, scatter, 0)
-    pltpu.make_async_copy(r2, r2, ex_recv.at[1]).wait()
-    ag[64 * core + chip] = pk[64 * core + chip] + jnp.sum(r2[...], axis=0)
-
-    def gather(d, carry):
-        device = peer(d)[1]
-        tile = ag.at[64 * core + chip]
-        pltpu.make_async_remote_copy(
-            src_ref=tile, dst_ref=tile, send_sem=ex_send.at[2], recv_sem=ex_recv.at[2],
-            device_id=device, device_id_type=MESH,
-        ).start()
-        return carry
-
-    lax.fori_loop(1, 64, gather, 0)
-    pltpu.make_async_copy(r2, r2, ex_recv.at[2]).wait()
-    swap = pltpu.make_async_remote_copy(
-        src_ref=ag.at[mine], dst_ref=ag.at[mine], send_sem=ex_send.at[3], recv_sem=ex_recv.at[3],
-        device_id=sibling, device_id_type=MESH,
-    )
-    swap.start()
-    swap.wait_recv()
+
+    def arrived(phase, ref):
+        pltpu.make_async_copy(ref, ref, ex_recv.at[phase]).wait()
+
+    half = pl.ds(64 * core, 64)
+    mine = 64 * core + 16 * xx + 4 * y + z
+    send(0, pk.at[pl.ds(64 * (1 - core), 64)], r1, sibling)
+    pl.semaphore_wait(line_sem.at[1], 3)
+    arrived(0, r1)
+    pk[half] += r1[...]
+    for n, steps in enumerate(others):
+        chip, device = peer(*steps)
+        send(1, pk.at[64 * core + chip], r2.at[n], device)
+    arrived(1, r2)
+    ag[mine] = pk[mine] + jnp.sum(r2[...], axis=0)
+    for steps in others:
+        send(2, ag.at[mine], ag.at[mine], peer(*steps)[1])
+    arrived(2, r2)
+    send(3, ag.at[half], ag.at[half], sibling)
+    arrived(3, r1)
     g_ref[...] = ag[...]
 
-    swap.wait_send()
-    pair.wait_send()
-    pltpu.make_async_copy(r2, r2, ex_send.at[1]).wait()
-    pltpu.make_async_copy(r2, r2, ex_send.at[2]).wait()
+    for phase, ref in enumerate((r1, r2, r2, r1)):
+        pltpu.make_async_copy(ref, ref, ex_send.at[phase]).wait()
 
     def sent(j, carry):
         for copy in halo(j):
@@ -420,12 +422,11 @@
     )(tiles, start.T, features)
 
 
-def on_device(radiance, counts, start):
-    x = radiance.reshape(BANDS * ROWS, COLS)
+def first(counts, x):
     vmem = pl.BlockSpec(memory_space=pltpu.VMEM)
     hbm = pl.BlockSpec(memory_space=pltpu.HBM)
     dma = pltpu.SemaphoreType.DMA
-    features, tiles = pl.pallas_call(
+    return pl.pallas_call(
         features_kernel,
         out_shape=(
             jax.ShapeDtypeStruct((BP, ROWS * COLS), BF16),
@@ -440,6 +441,10 @@
             pltpu.VMEM((HR, COLS), BF16),
             pltpu.VMEM((HR, COLS), BF16),
             pltpu.VMEM((BP, ROWS * COLS), BF16),
+            pltpu.VMEM((192 * CHUNK, COLS), BF16),
+            pltpu.VMEM((192 * CHUNK, COLS), BF16),
+            pltpu.VMEM((768, 256), BF16),
+            pltpu.VMEM((512, 128), BF16),
             pltpu.VMEM((4, BP, COLS), F32),
             pltpu.VMEM((BP, 512), F32),
             pltpu.VMEM((128, 8, 128), F32),
@@ -454,11 +459,17 @@
             dma((CHUNKS,)),
             dma((4,)),
             dma((4,)),
+            pltpu.SemaphoreType.REGULAR((2,)),
         ],
         compiler_params=pltpu.CompilerParams(
             collective_id=0, has_side_effects=True, vmem_limit_bytes=56 * 2**20
         ),
     )(counts, x)
+
+
+def on_device(radiance, counts, start):
+    x = radiance.reshape(BANDS * ROWS, COLS)
+    features, tiles = first(counts, x)
     projector, scores = second(tiles, start, features)
     return projector, scores.reshape(1, RANK, ROWS, COLS)
 

time: 80.7 us -> 68.4 us (0.85)
  Pallas kernels: 79.3 us -> 67 us
    pallas_call x1, Pallas kernels: 55.1 us -> 42.8 us  [first(): pl.pallas_call(features_kernel, out_shape=(jax.ShapeDtypeStruct((BP, ROWS...]
where the time goes in v3:
time: 68.4 us; the launch traced here: 68.3 us
  Pallas kernels  67 us (98%)
  between operations  1.28 us (2%)
    pallas_call x1, Pallas kernels, first(): pl.pallas_call(features_kernel, out_shape=(jax.ShapeDtypeStruct((BP, ROWS...  42.8 us
    pallas_call x1, Pallas kernels, second(): pl.pallas_call(iterate_kernel, out_shape=(jax.ShapeDtypeStruct((BANDS, BA...  24.2 us

profile of v3, /device:TPU:1, one launch (start us, length us, event | category | flops | bytes accessed | tf_op | source)
XLA Modules:
  0.0 68.3 jit_solution(7005314077305488344)
XLA Ops:
  1.3 42.8 %shard_map.50 = (bf16[432,6144]{1,0:T(8,128)(2,1)}, f32[128,8,128]{2,1,0:T(8,128)}) custom-call(s32[1,1]{1,0:T(1,128)S(6)} %copy.5.counts_ref, bf16[6800,384]{1,0:T(8,128)(2,1)} %bitcast.3), custom_call_target="tpu_custom_call" | custom-call | tf_op jit(solution)/shard_map/pallas_call | solution.py:429
  44.1 24.2 %shard_map.51 = (f32[425,425]{1,0:T(8,128)}, f32[1024,384]{1,0:T(8,128)}) custom-call(f32[128,8,128]{2,1,0:T(8,128)} %get-tuple-element.6.g_ref, f32[64,425]{1,0:T(8,128)} %bitcast.4, bf16[432,6144]{1,0:T(8,128)(2,1)} %get-tuple-element.7.f_hbm), custom_call_target="tpu_custom_call" | custom-call | tf_op jit(solution)/shard_map/pallas_call | solution.py:402

commit v4 on v3

--- a/solution.py
+++ b/solution.py
@@ -53,10 +53,77 @@
     )
 
 
+def split3(a):
+    hi = a.astype(BF16)
+    rest = a - hi.astype(F32)
+    mid = rest.astype(BF16)
+    low = (rest - mid.astype(F32)).astype(BF16)
+    return hi, mid, low
+
+
+def dot6(a, b, dims):
+    n = a.shape[0]
+    parts = jnp.concatenate(split3(a), axis=0)
+    one = lax.dot_general(parts, b[0], dims, preferred_element_type=F32)
+    two = lax.dot_general(parts[: 2 * n], b[1], dims, preferred_element_type=F32)
+    three = lax.dot_general(parts[:n], b[2], dims, preferred_element_type=F32)
+    return one[:n] + (((one[2 * n :] + two[n:]) + three) + (one[n : 2 * n] + two[:n]))
+
+
+NN = (((1,), (0,)), ((), ()))
+
+
+def inverse_factor(s):
+    ri, ci = iotas((8, 128))
+    spread = lambda v, k: jnp.broadcast_to(v[k : k + 1], (8, 128))
+    rows = [s[8 * i : 8 * i + 8] + (ci == ri + 64 + 8 * i).astype(F32) for i in range(8)]
+
+    def columns(p, i):
+        return [jnp.broadcast_to(rows[i][:, 8 * p + l : 8 * p + l + 1], (8, 128)) for l in range(8)]
+
+    ahead = columns(0, 0)
+    for p in range(8):
+        pivots = jnp.ones((8, 128), F32)
+        cols, steps = ahead + (columns(p + 1, p) if p < 7 else []), []
+        width = len(cols)
+        for k in range(8):
+            pivot = spread(cols[k], k)
+            pivots = jnp.where(ri == k, pivot, pivots)
+            inv = 1.0 / pivot
+            heads = [spread(cols[l], k) * inv for l in range(k + 1, width)]
+            row = spread(rows[p], k) * inv
+            steps.append((heads, row))
+            if k < 7:
+                m = jnp.where(ri > k, cols[k], 0.0)
+                for l in range(k + 1, width):
+                    cols[l] = cols[l] - m * heads[l - k - 1]
+                rows[p] = rows[p] - m * row
+        for i in range(p + 1, 8):
+            cols = columns(p, i) + (columns(p + 1, i) if i == p + 1 else [])
+            for k, (heads, row) in enumerate(steps):
+                for l in range(k + 1, len(cols)):
+                    cols[l] = cols[l] - cols[k] * heads[l - k - 1]
+                rows[i] = rows[i] - cols[k] * row
+            if i == p + 1:
+                ahead = cols[8:]
+        rows[p] = rows[p] * lax.rsqrt(pivots)
+    return jnp.concatenate(rows, axis=0)
+
+
+def normaliser(t):
+    zeros = jnp.zeros((RANK, 512), BF16)
+    return inverse_factor(dot6(t, tuple(jnp.concatenate([p, zeros], axis=0) for p in split3(t)), NT))
+
+
+def apply(w, t):
+    zeros = jnp.zeros((RANK, 512), BF16)
+    return dot6(w, tuple(jnp.concatenate([zeros, p], axis=0) for p in split3(t)), NN)
+
+
 def features_kernel(
-    counts_ref, x_hbm, f_hbm, g_ref,
-    xs, su, sd, hu, hd, fs, th, tl, wl, wr, tb, gs, pk, r1, r2, ag,
-    x_sem, f_sem, su_sem, sd_sem, hu_sem, hd_sem, ex_send, ex_recv, line_sem,
+    counts_ref, x_hbm, start_hbm, f_hbm, g_ref, b_ref,
+    xs, su, sd, hu, hd, fs, th, tl, wl, wr, tb, gs, pk, r1, r2, ag, st,
+    x_sem, f_sem, su_sem, sd_sem, hu_sem, hd_sem, ex_send, ex_recv, line_sem, st_sem,
 ):
     line, track = lax.axis_index("line"), lax.axis_index("track")
     y, core = line // 2, line % 2
@@ -87,6 +154,8 @@
 
     for j in range(CHUNKS):
         load(j).start()
+    st_copy = pltpu.make_async_copy(start_hbm, st, st_sem)
+    st_copy.start()
 
     barrier = pltpu.get_barrier_semaphore()
     for device in greeted:
@@ -217,8 +286,10 @@
     for copy in halo(0):
         copy.wait_recv()
     edges(0, CHUNK - 1)
-    lax.fori_loop(1, CHUNKS, edge_step, 0)
-    edges(GROUPS - 1, 1)
+    lax.fori_loop(1, CHUNKS - 1, edge_step, 0)
+    for copy in halo(CHUNKS - 1):
+        copy.wait_recv()
+    edges(GROUPS - CHUNK - 1, CHUNK + 1)
 
     f_copy = pltpu.make_async_copy(fs, f_hbm, f_sem)
     f_copy.start()
@@ -251,6 +322,9 @@
     for n, steps in enumerate(others):
         chip, device = peer(*steps)
         send(1, pk.at[64 * core + chip], r2.at[n], device)
+    st_copy.wait()
+    begin = jnp.concatenate([st[...], jnp.zeros((RANK, 512 - BANDS), F32)], axis=1)
+    b_ref[...] = apply(normaliser(begin), begin)
     arrived(1, r2)
     ag[mine] = pk[mine] + jnp.sum(r2[...], axis=0)
     for steps in others:
@@ -272,58 +346,7 @@
     f_copy.wait()
 
 
-def split3(a):
-    hi = a.astype(BF16)
-    rest = a - hi.astype(F32)
-    mid = rest.astype(BF16)
-    low = (rest - mid.astype(F32)).astype(BF16)
-    return hi, mid, low
-
-
-def dot6(a, b, dims):
-    n = a.shape[0]
-    parts = jnp.concatenate(split3(a), axis=0)
-    one = lax.dot_general(parts, b[0], dims, preferred_element_type=F32)
-    two = lax.dot_general(parts[: 2 * n], b[1], dims, preferred_element_type=F32)
-    three = lax.dot_general(parts[:n], b[2], dims, preferred_element_type=F32)
-    return one[:n] + (((one[2 * n :] + two[n:]) + three) + (one[n : 2 * n] + two[:n]))
-
-
-NN = (((1,), (0,)), ((), ()))
-
-
-def reciprocal(d):
-    return 1.0 / d
-
-
-def inverse_factor(s):
-    ri, ci = iotas((8, 128))
-    rows = [s[8 * i : 8 * i + 8] + (ci == ri + 64 + 8 * i).astype(F32) for i in range(8)]
-    spread = lambda v, k: jnp.broadcast_to(v[k : k + 1], (8, 128))
-    for p in range(8):
-        cols = {
-            i: [jnp.broadcast_to(rows[i][:, 8 * p + l : 8 * p + l + 1], (8, 128)) for l in range(8)]
-            for i in range(p, 8)
-        }
-        pivots = jnp.ones((8, 128), F32)
-        for k in range(8):
-            pivot = spread(cols[p][k], k)
-            pivots = jnp.where(ri == k, pivot, pivots)
-            inv = reciprocal(pivot)
-            heads = [spread(cols[p][l], k) * inv for l in range(k + 1, 8)]
-            row = spread(rows[p], k) * inv
-            for i in range(p, 8):
-                if i == p and k == 7:
-                    continue
-                m = jnp.where(ri > k, cols[i][k], 0.0) if i == p else cols[i][k]
-                for l in range(k + 1, 8):
-                    cols[i][l] = cols[i][l] - m * heads[l - k - 1]
-                rows[i] = rows[i] - m * row
-        rows[p] = rows[p] * lax.rsqrt(pivots)
-    return jnp.concatenate(rows, axis=0)
-
-
-def iterate_kernel(g_ref, start_ref, f_hbm, proj_ref, scores_hbm, gf, gh, gm, gl, tt, fs, sc, f_sem, o_sem):
+def iterate_kernel(g_ref, first_ref, f_hbm, proj_ref, scores_hbm, gf, gh, gm, gl, tt, fs, sc, f_sem, o_sem):
     f_copy = pltpu.make_async_copy(f_hbm, fs, f_sem)
     f_copy.start()
 
@@ -342,19 +365,7 @@
     for ref, part in zip((gh, gm, gl), split3(gf[...])):
         ref[...] = part
 
-    tt[:, 384:512] = jnp.zeros((RANK, 128), F32)
-    tt[:, 0:BANDS] = start_ref[...]
-
-    zeros = jnp.zeros((RANK, 512), BF16)
-
-    def normaliser(t):
-        h, m, l = split3(t)
-        rhs = tuple(jnp.concatenate([p, zeros], axis=0) for p in (h, m, l))
-        return inverse_factor(dot6(t, rhs, NT))
-
-    def apply(w, t):
-        rhs = tuple(jnp.concatenate([zeros, p], axis=0) for p in split3(t))
-        return dot6(w, rhs, NN)
+    tt[...] = dot6(first_ref[...], (gh[...], gm[...], gl[...]), NN)
 
     def step(i, carry):
         t = tt[...]
@@ -362,7 +373,7 @@
         tt[...] = apply(normaliser(t), z)
         return carry
 
-    lax.fori_loop(0, ITERS, step, 0)
+    lax.fori_loop(1, ITERS, step, 0)
     t = tt[...]
     basis = apply(normaliser(t), t)
 
@@ -375,27 +386,23 @@
     f_copy.wait()
     narrow = h[:, 0:BP]
 
-    def score(r, carry):
-        cols = pl.ds(pl.multiple_of(r * COLS, 128), COLS)
-        s = jnp.dot(narrow, fs[:, cols], preferred_element_type=F32)
-        for i in range(3):
-            sc[pl.ds(RANK * ROWS * i + r, RANK, stride=ROWS), :] = s[:, 128 * i : 128 * i + 128]
-        return carry
-
-    lax.fori_loop(0, ROWS, score, 0)
     out = [
         pltpu.make_async_copy(
             sc.at[pl.ds(RANK * ROWS * i, RANK * ROWS)], scores_hbm.at[:, pl.ds(128 * i, 128)], o_sem.at[i]
         )
         for i in range(3)
     ]
-    for copy in out:
-        copy.start()
+    for i in range(3):
+        for r in range(ROWS):
+            col = r * COLS + 128 * i
+            part = jnp.dot(narrow, fs[:, col : col + 128], preferred_element_type=F32)
+            sc[pl.ds(RANK * ROWS * i + r, RANK, stride=ROWS), :] = part
+        out[i].start()
     for copy in out:
         copy.wait()
 
 
-def second(tiles, start, features):
+def second(tiles, begin, features):
     vmem = pl.BlockSpec(memory_space=pltpu.VMEM)
     hbm = pl.BlockSpec(memory_space=pltpu.HBM)
     dma = pltpu.SemaphoreType.DMA
@@ -418,11 +425,11 @@
             dma,
             dma((3,)),
         ],
-        compiler_params=pltpu.CompilerParams(vmem_limit_bytes=56 * 2**20),
-    )(tiles, start.T, features)
-
-
-def first(counts, x):
+        compiler_params=pltpu.CompilerParams(vmem_limit_bytes=53 * 2**20),
+    )(tiles, begin, features)
+
+
+def first(counts, x, start):
     vmem = pl.BlockSpec(memory_space=pltpu.VMEM)
     hbm = pl.BlockSpec(memory_space=pltpu.HBM)
     dma = pltpu.SemaphoreType.DMA
@@ -431,9 +438,10 @@
         out_shape=(
             jax.ShapeDtypeStruct((BP, ROWS * COLS), BF16),
             jax.ShapeDtypeStruct((128, 8, 128), F32),
+            jax.ShapeDtypeStruct((RANK, 512), F32),
         ),
-        in_specs=[pl.BlockSpec(memory_space=pltpu.SMEM), hbm],
-        out_specs=(hbm, vmem),
+        in_specs=[pl.BlockSpec(memory_space=pltpu.SMEM), hbm, hbm],
+        out_specs=(hbm, vmem, vmem),
         scratch_shapes=[
             pltpu.VMEM((ROWS * (BP + 2), COLS), BF16),
             pltpu.VMEM((HR, COLS), BF16),
@@ -451,6 +459,7 @@
             pltpu.VMEM((64, 8, 128), F32),
             pltpu.VMEM((63, 8, 128), F32),
             pltpu.VMEM((128, 8, 128), F32),
+            pltpu.VMEM((RANK, BANDS), F32),
             dma((CHUNKS,)),
             dma,
             dma((CHUNKS,)),
@@ -460,17 +469,18 @@
             dma((4,)),
             dma((4,)),
             pltpu.SemaphoreType.REGULAR((2,)),
+            dma,
         ],
         compiler_params=pltpu.CompilerParams(
-            collective_id=0, has_side_effects=True, vmem_limit_bytes=56 * 2**20
+            collective_id=0, has_side_effects=True, vmem_limit_bytes=53 * 2**20
         ),
-    )(counts, x)
+    )(counts, x, start.T)
 
 
 def on_device(radiance, counts, start):
     x = radiance.reshape(BANDS * ROWS, COLS)
-    features, tiles = first(counts, x)
-    projector, scores = second(tiles, start, features)
+    features, tiles, begin = first(counts, x, start)
+    projector, scores = second(tiles, begin, features)
     return projector, scores.reshape(1, RANK, ROWS, COLS)
 
 

time: 68.4 us -> 60.3 us (0.88)
  Pallas kernels: 67 us -> 57.9 us
  local copies, waits for them, and re-layouts: 0 us -> 0.9 us
    pallas_call x1, Pallas kernels: 24.2 us -> 16.2 us  [second(): pl.pallas_call(iterate_kernel, out_shape=(jax.ShapeDtypeStruct((BANDS, BA...]
    pallas_call x1, Pallas kernels: 42.8 us -> 41.7 us  [first(): pl.pallas_call(features_kernel, out_shape=(jax.ShapeDtypeStruct((BP, ROWS...]
    unnamed x0 -> x2, local copies, waits for them, and re-layouts: none -> 0.9 us
where the time goes in v4:
time: 60.3 us; the launch traced here: 60.2 us
  Pallas kernels  57.9 us (96%)
  between operations  1.45 us (2%)
  local copies, waits for them, and re-layouts  0.9 us (1%)
    pallas_call x1, Pallas kernels, first(): pl.pallas_call(features_kernel, out_shape=(jax.ShapeDtypeStruct((BP, ROWS...  41.7 us
    pallas_call x1, Pallas kernels, second(): pl.pallas_call(iterate_kernel, out_shape=(jax.ShapeDtypeStruct((BANDS, BA...  16.2 us

profile of v4, /device:TPU:1, one launch (start us, length us, event | category | flops | bytes accessed | tf_op | source)
XLA Modules:
  0.0 60.2 jit_solution(18271490775520141648)
XLA Ops:
  1.3 0.0 copy-start
  1.3 0.9 %copy-done = f32[425,64]{0,1:T(8,128)S(1)} copy-done((f32[425,64]{0,1:T(8,128)S(1)}, f32[425,64]{0,1:T(8,128)}, u32[]{:S(2)}) %copy-start) | copy-done | bytes 108824
  2.2 41.7 %shard_map.50 = (bf16[432,6144]{1,0:T(8,128)(2,1)}, f32[128,8,128]{2,1,0:T(8,128)S(1)}, f32[64,512]{1,0:T(8,128)S(1)}) custom-call(s32[1,1]{1,0:T(1,128)S(6)} %copy.5.counts_ref, bf16[6800,384]{1,0:T(8,128)(2,1)} %bitcast.4, f32[64,425]{1,0:T(8,128)S(1)} %bitcast.3), custom_call_target="tpu_custom_call" | custom-call | tf_op jit(solution)/shard_map/pallas_call | solution.py:436
  43.9 16.2 %shard_map.51 = (f32[425,425]{1,0:T(8,128)}, f32[1024,384]{1,0:T(8,128)}) custom-call(f32[128,8,128]{2,1,0:T(8,128)S(1)} %get-tuple-element.7.g_ref, f32[64,512]{1,0:T(8,128)S(1)} %get-tuple-element.8.first_ref, bf16[432,6144]{1,0:T(8,128)(2,1)} %get-tuple-element.9.f_hbm), custom_call_target="tpu_custom_call" | custom-call | tf_op jit(solution)/shard_map/pallas_call | solution.py:409
Async XLA Ops:
  1.3 0.9 %copy-start = (f32[425,64]{0,1:T(8,128)S(1)}, f32[425,64]{0,1:T(8,128)}, u32[]{:S(2)}) copy-start(f32[425,64]{0,1:T(8,128)} %param.5) | copy-start | bytes 326404

commit v5 on v4

--- a/solution.py
+++ b/solution.py
@@ -21,6 +21,7 @@
 TILES = 16
 CHUNK = 3
 CHUNKS = GROUPS // CHUNK
+SENT = [CHUNK] * (CHUNKS - 1) + [CHUNK - 1, 1]
 HR = 16 + 2 * BP + 16
 EDGE = (0, 1, 14, 15)
 BIN = lambda dist: jnp.where(dist == 0, 6.0, jnp.where(dist == 1, 4.0, jnp.where(dist == 2, 1.0, 0.0)))
@@ -174,7 +175,10 @@
     sel = ((((ri & 31) >> 1) == (ci >> 4)) & (want == (ci & 15)) & (want < cnt)).astype(F32).astype(BF16)
 
     def halo(j):
-        rows = pl.ds(pl.multiple_of(16 + 32 * CHUNK * j, 32 * CHUNK // 6), 32 * CHUNK)
+        if isinstance(j, int):
+            rows = pl.ds(16 + 32 * sum(SENT[:j]), 32 * SENT[j])
+        else:
+            rows = pl.ds(pl.multiple_of(16 + 32 * CHUNK * j, 16), 32 * CHUNK)
         first = pltpu.make_async_remote_copy(
             src_ref=su.at[rows], dst_ref=hd.at[rows], send_sem=su_sem.at[j], recv_sem=hd_sem.at[j],
             device_id=before, device_id_type=MESH,
@@ -185,9 +189,10 @@
         )
         return first, last
 
-    for j in range(CHUNKS):
-        load(j).wait()
-        for g in range(CHUNK * j, CHUNK * j + CHUNK):
+    for j in range(len(SENT)):
+        if j < CHUNKS:
+            load(j).wait()
+        for g in range(sum(SENT[:j]), sum(SENT[: j + 1])):
             picked = jnp.dot(sel, xs[16 + 256 * g : 272 + 256 * g, :], preferred_element_type=F32).astype(BF16)
             su[16 + 32 * g : 48 + 32 * g, :] = picked[0:32]
             sd[16 + 32 * g : 48 + 32 * g, :] = picked[32:64]
@@ -289,7 +294,10 @@
     lax.fori_loop(1, CHUNKS - 1, edge_step, 0)
     for copy in halo(CHUNKS - 1):
         copy.wait_recv()
-    edges(GROUPS - CHUNK - 1, CHUNK + 1)
+    edges(GROUPS - CHUNK - 1, 2)
+    for copy in halo(CHUNKS):
+        copy.wait_recv()
+    edges(GROUPS - 2, 2)
 
     f_copy = pltpu.make_async_copy(fs, f_hbm, f_sem)
     f_copy.start()
@@ -342,11 +350,13 @@
             copy.wait_send()
         return carry
 
-    lax.fori_loop(0, CHUNKS, sent, 0)
+    lax.fori_loop(0, CHUNKS - 1, sent, 0)
+    for j in (CHUNKS - 1, CHUNKS):
+        sent(j, 0)
     f_copy.wait()
 
 
-def iterate_kernel(g_ref, first_ref, f_hbm, proj_ref, scores_hbm, gf, gh, gm, gl, tt, fs, sc, f_sem, o_sem):
+def iterate_kernel(g_ref, first_ref, f_hbm, proj_hbm, scores_hbm, gf, gh, gm, gl, tt, fs, sc, pj, f_sem, o_sem, p_sem):
     f_copy = pltpu.make_async_copy(f_hbm, fs, f_sem)
     f_copy.start()
 
@@ -381,7 +391,9 @@
     lhs = jnp.concatenate([h, h, m, m], axis=0).astype(F32).T.astype(BF16)
     rhs = jnp.concatenate([h, m, h, m], axis=0)
     proj = jnp.dot(lhs, rhs, preferred_element_type=F32)
-    proj_ref[...] = proj[0:BANDS, 0:BANDS]
+    pj[...] = proj[0:BANDS, 0:BANDS]
+    p_copy = pltpu.make_async_copy(pj, proj_hbm, p_sem)
+    p_copy.start()
 
     f_copy.wait()
     narrow = h[:, 0:BP]
@@ -400,6 +412,7 @@
         out[i].start()
     for copy in out:
         copy.wait()
+    p_copy.wait()
 
 
 def second(tiles, begin, features):
@@ -413,7 +426,7 @@
             jax.ShapeDtypeStruct((RANK * ROWS, COLS), F32),
         ),
         in_specs=[vmem, vmem, hbm],
-        out_specs=(vmem, hbm),
+        out_specs=(hbm, hbm),
         scratch_shapes=[
             pltpu.VMEM((512, 512), F32),
             pltpu.VMEM((512, 512), BF16),
@@ -422,8 +435,10 @@
             pltpu.VMEM((RANK, 512), F32),
             pltpu.VMEM((BP, ROWS * COLS), BF16),
             pltpu.VMEM((3 * RANK * ROWS, 128), F32),
+            pltpu.VMEM((BANDS, BANDS), F32),
             dma,
             dma((3,)),
+            dma,
         ],
         compiler_params=pltpu.CompilerParams(vmem_limit_bytes=53 * 2**20),
     )(tiles, begin, features)
@@ -462,10 +477,10 @@
             pltpu.VMEM((RANK, BANDS), F32),
             dma((CHUNKS,)),
             dma,
-            dma((CHUNKS,)),
-            dma((CHUNKS,)),
-            dma((CHUNKS,)),
-            dma((CHUNKS,)),
+            dma((CHUNKS + 1,)),
+            dma((CHUNKS + 1,)),
+            dma((CHUNKS + 1,)),
+            dma((CHUNKS + 1,)),
             dma((4,)),
             dma((4,)),
             pltpu.SemaphoreType.REGULAR((2,)),

time: 60.3 us -> 59.5 us (0.987)
  Pallas kernels: 57.9 us -> 57 us
    pallas_call x1, Pallas kernels: 16.2 us -> 15.3 us  [second(): pl.pallas_call(iterate_kernel, out_shape=(jax.ShapeDtypeStruct((BANDS, BA...]
where the time goes in v5:
time: 59.5 us; the launch traced here: 59.3 us
  Pallas kernels  57 us (96%)
  between operations  1.45 us (2%)
  local copies, waits for them, and re-layouts  0.9 us (2%)
    pallas_call x1, Pallas kernels, first(): pl.pallas_call(features_kernel, out_shape=(jax.ShapeDtypeStruct((BP, ROWS...  41.7 us
    pallas_call x1, Pallas kernels, second(): pl.pallas_call(iterate_kernel, out_shape=(jax.ShapeDtypeStruct((BANDS, BA...  15.3 us

profile of v5, /device:TPU:1, one launch (start us, length us, event | category | flops | bytes accessed | tf_op | source)
XLA Modules:
  0.0 59.3 jit_solution(6432092595208298159)
XLA Ops:
  1.3 0.0 copy-start
  1.3 0.9 %copy-done = f32[425,64]{0,1:T(8,128)S(1)} copy-done((f32[425,64]{0,1:T(8,128)S(1)}, f32[425,64]{0,1:T(8,128)}, u32[]{:S(2)}) %copy-start) | copy-done | bytes 108824
  2.2 41.7 %shard_map.50 = (bf16[432,6144]{1,0:T(8,128)(2,1)}, f32[128,8,128]{2,1,0:T(8,128)S(1)}, f32[64,512]{1,0:T(8,128)S(1)}) custom-call(s32[1,1]{1,0:T(1,128)S(6)} %copy.5.counts_ref, bf16[6800,384]{1,0:T(8,128)(2,1)} %bitcast.4, f32[64,425]{1,0:T(8,128)S(1)} %bitcast.3), custom_call_target="tpu_custom_call" | custom-call | tf_op jit(solution)/shard_map/pallas_call | solution.py:451
  43.9 15.3 %shard_map.51 = (f32[425,425]{1,0:T(8,128)}, f32[1024,384]{1,0:T(8,128)}) custom-call(f32[128,8,128]{2,1,0:T(8,128)S(1)} %get-tuple-element.7.g_ref, f32[64,512]{1,0:T(8,128)S(1)} %get-tuple-element.8.first_ref, bf16[432,6144]{1,0:T(8,128)(2,1)} %get-tuple-element.9.f_hbm), custom_call_target="tpu_custom_call" | custom-call | tf_op jit(solution)/shard_map/pallas_call | solution.py:422
Async XLA Ops:
  1.3 0.9 %copy-start = (f32[425,64]{0,1:T(8,128)S(1)}, f32[425,64]{0,1:T(8,128)}, u32[]{:S(2)}) copy-start(f32[425,64]{0,1:T(8,128)} %param.5) | copy-start | bytes 326404

commit v6 on v5

--- a/solution.py
+++ b/solution.py
@@ -80,7 +80,10 @@
     rows = [s[8 * i : 8 * i + 8] + (ci == ri + 64 + 8 * i).astype(F32) for i in range(8)]
 
     def columns(p, i):
-        return [jnp.broadcast_to(rows[i][:, 8 * p + l : 8 * p + l + 1], (8, 128)) for l in range(8)]
+        return [
+            jnp.take_along_axis(rows[i], jnp.full((8, 128), 8 * p + l, jnp.int32), axis=1, mode="promise_in_bounds")
+            for l in range(8)
+        ]
 
     ahead = columns(0, 0)
     for p in range(8):
@@ -111,9 +114,9 @@
     return jnp.concatenate(rows, axis=0)
 
 
-def normaliser(t):
+def inner(t):
     zeros = jnp.zeros((RANK, 512), BF16)
-    return inverse_factor(dot6(t, tuple(jnp.concatenate([p, zeros], axis=0) for p in split3(t)), NT))
+    return dot6(t, tuple(jnp.concatenate([p, zeros], axis=0) for p in split3(t)), NT)
 
 
 def apply(w, t):
@@ -332,7 +335,7 @@
         send(1, pk.at[64 * core + chip], r2.at[n], device)
     st_copy.wait()
     begin = jnp.concatenate([st[...], jnp.zeros((RANK, 512 - BANDS), F32)], axis=1)
-    b_ref[...] = apply(normaliser(begin), begin)
+    b_ref[...] = apply(inverse_factor(inner(begin)), begin)
     arrived(1, r2)
     ag[mine] = pk[mine] + jnp.sum(r2[...], axis=0)
     for steps in others:
@@ -379,13 +382,14 @@
 
     def step(i, carry):
         t = tt[...]
+        s = inner(t)
         z = dot6(t, (gh[...], gm[...], gl[...]), NN)
-        tt[...] = apply(normaliser(t), z)
+        tt[...] = apply(inverse_factor(s), z)
         return carry
 
     lax.fori_loop(1, ITERS, step, 0)
     t = tt[...]
-    basis = apply(normaliser(t), t)
+    basis = apply(inverse_factor(inner(t)), t)
 
     h, m, l = split3(basis)
     lhs = jnp.concatenate([h, h, m, m], axis=0).astype(F32).T.astype(BF16)

time: 59.5 us -> 57.2 us (0.961)
  Pallas kernels: 57 us -> 54.7 us
    pallas_call x1, Pallas kernels: 15.3 us -> 13 us  [second(): pl.pallas_call(iterate_kernel, out_shape=(jax.ShapeDtypeStruct((BANDS, BA...]
where the time goes in v6:
time: 57.2 us; the launch traced here: 57.1 us
  Pallas kernels  54.7 us (96%)
  between operations  1.45 us (3%)
  local copies, waits for them, and re-layouts  0.9 us (2%)
    pallas_call x1, Pallas kernels, first(): pl.pallas_call(features_kernel, out_shape=(jax.ShapeDtypeStruct((BP, ROWS...  41.7 us
    pallas_call x1, Pallas kernels, second(): pl.pallas_call(iterate_kernel, out_shape=(jax.ShapeDtypeStruct((BANDS, BA...  13 us

profile of v6, /device:TPU:1, one launch (start us, length us, event | category | flops | bytes accessed | tf_op | source)
XLA Modules:
  0.0 57.1 jit_solution(984154796265248207)
XLA Ops:
  1.3 0.0 copy-start
  1.3 0.9 %copy-done = f32[425,64]{0,1:T(8,128)S(1)} copy-done((f32[425,64]{0,1:T(8,128)S(1)}, f32[425,64]{0,1:T(8,128)}, u32[]{:S(2)}) %copy-start) | copy-done | bytes 108824
  2.2 41.7 %shard_map.50 = (bf16[432,6144]{1,0:T(8,128)(2,1)}, f32[128,8,128]{2,1,0:T(8,128)S(1)}, f32[64,512]{1,0:T(8,128)S(1)}) custom-call(s32[1,1]{1,0:T(1,128)S(6)} %copy.5.counts_ref, bf16[6800,384]{1,0:T(8,128)(2,1)} %bitcast.4, f32[64,425]{1,0:T(8,128)S(1)} %bitcast.3), custom_call_target="tpu_custom_call" | custom-call | tf_op jit(solution)/shard_map/pallas_call | solution.py:455
  43.9 13.0 %shard_map.51 = (f32[425,425]{1,0:T(8,128)}, f32[1024,384]{1,0:T(8,128)}) custom-call(f32[128,8,128]{2,1,0:T(8,128)S(1)} %get-tuple-element.7.g_ref, f32[64,512]{1,0:T(8,128)S(1)} %get-tuple-element.8.first_ref, bf16[432,6144]{1,0:T(8,128)(2,1)} %get-tuple-element.9.f_hbm), custom_call_target="tpu_custom_call" | custom-call | tf_op jit(solution)/shard_map/pallas_call | solution.py:426
Async XLA Ops:
  1.3 0.9 %copy-start = (f32[425,64]{0,1:T(8,128)S(1)}, f32[425,64]{0,1:T(8,128)}, u32[]{:S(2)}) copy-start(f32[425,64]{0,1:T(8,128)} %param.5) | copy-start | bytes 326404

commit v7 on v6

--- a/solution.py
+++ b/solution.py
@@ -94,20 +94,23 @@
             pivot = spread(cols[k], k)
             pivots = jnp.where(ri == k, pivot, pivots)
             inv = 1.0 / pivot
-            heads = [spread(cols[l], k) * inv for l in range(k + 1, width)]
-            row = spread(rows[p], k) * inv
-            steps.append((heads, row))
+            heads = [spread(cols[l], k) for l in range(k + 1, width)]
+            row = spread(rows[p], k)
+            steps.append((heads, row, inv))
             if k < 7:
-                m = jnp.where(ri > k, cols[k], 0.0)
-                for l in range(k + 1, width):
+                under = jnp.where(ri > k, cols[k], 0.0)
+                m = under * inv
+                cols[k + 1] = cols[k + 1] - (under * heads[0]) * inv
+                for l in range(k + 2, width):
                     cols[l] = cols[l] - m * heads[l - k - 1]
                 rows[p] = rows[p] - m * row
         for i in range(p + 1, 8):
             cols = columns(p, i) + (columns(p + 1, i) if i == p + 1 else [])
-            for k, (heads, row) in enumerate(steps):
+            for k, (heads, row, inv) in enumerate(steps):
+                m = cols[k] * inv
                 for l in range(k + 1, len(cols)):
-                    cols[l] = cols[l] - cols[k] * heads[l - k - 1]
-                rows[i] = rows[i] - cols[k] * row
+                    cols[l] = cols[l] - m * heads[l - k - 1]
+                rows[i] = rows[i] - m * row
             if i == p + 1:
                 ahead = cols[8:]
         rows[p] = rows[p] * lax.rsqrt(pivots)

time: 57.2 us -> 56.4 us (0.986)
  Pallas kernels: 54.7 us -> 54.1 us
    pallas_call x1, Pallas kernels: 13 us -> 12.3 us  [second(): pl.pallas_call(iterate_kernel, out_shape=(jax.ShapeDtypeStruct((BANDS, BA...]
where the time goes in v7:
time: 56.4 us; the launch traced here: 56.3 us
  Pallas kernels  54.1 us (96%)
  between operations  1.29 us (2%)
  local copies, waits for them, and re-layouts  0.9 us (2%)
    pallas_call x1, Pallas kernels, first(): pl.pallas_call(features_kernel, out_shape=(jax.ShapeDtypeStruct((BP, ROWS...  41.7 us
    pallas_call x1, Pallas kernels, second(): pl.pallas_call(iterate_kernel, out_shape=(jax.ShapeDtypeStruct((BANDS, BA...  12.3 us

profile of v7, /device:TPU:1, one launch (start us, length us, event | category | flops | bytes accessed | tf_op | source)
XLA Modules:
  0.0 56.3 jit_solution(3384288634594175899)
XLA Ops:
  1.3 0.0 copy-start
  1.3 0.9 %copy-done = f32[425,64]{0,1:T(8,128)S(1)} copy-done((f32[425,64]{0,1:T(8,128)S(1)}, f32[425,64]{0,1:T(8,128)}, u32[]{:S(2)}) %copy-start) | copy-done | bytes 108824
  2.2 41.7 %shard_map.50 = (bf16[432,6144]{1,0:T(8,128)(2,1)}, f32[128,8,128]{2,1,0:T(8,128)S(1)}, f32[64,512]{1,0:T(8,128)S(1)}) custom-call(s32[1,1]{1,0:T(1,128)S(6)} %copy.5.counts_ref, bf16[6800,384]{1,0:T(8,128)(2,1)} %bitcast.4, f32[64,425]{1,0:T(8,128)S(1)} %bitcast.3), custom_call_target="tpu_custom_call" | custom-call | tf_op jit(solution)/shard_map/pallas_call | solution.py:458
  43.9 12.3 %shard_map.51 = (f32[425,425]{1,0:T(8,128)}, f32[1024,384]{1,0:T(8,128)}) custom-call(f32[128,8,128]{2,1,0:T(8,128)S(1)} %get-tuple-element.7.g_ref, f32[64,512]{1,0:T(8,128)S(1)} %get-tuple-element.8.first_ref, bf16[432,6144]{1,0:T(8,128)(2,1)} %get-tuple-element.9.f_hbm), custom_call_target="tpu_custom_call" | custom-call | tf_op jit(solution)/shard_map/pallas_call | solution.py:429
Async XLA Ops:
  1.3 0.9 %copy-start = (f32[425,64]{0,1:T(8,128)S(1)}, f32[425,64]{0,1:T(8,128)}, u32[]{:S(2)}) copy-start(f32[425,64]{0,1:T(8,128)} %param.5) | copy-start | bytes 326404

commit v8 on v7

--- a/solution.py
+++ b/solution.py
@@ -128,7 +128,7 @@
 
 
 def features_kernel(
-    counts_ref, x_hbm, start_hbm, f_hbm, g_ref, b_ref,
+    counts_ref, x_hbm, start_hbm, f_hbm, g0, g1, g2, g3, b_ref,
     xs, su, sd, hu, hd, fs, th, tl, wl, wr, tb, gs, pk, r1, r2, ag, st,
     x_sem, f_sem, su_sem, sd_sem, hu_sem, hd_sem, ex_send, ex_recv, line_sem, st_sem,
 ):
@@ -346,7 +346,8 @@
     arrived(2, r2)
     send(3, ag.at[half], ag.at[half], sibling)
     arrived(3, r1)
-    g_ref[...] = ag[...]
+    for n, out in enumerate((g0, g1, g2, g3)):
+        out[...] = ag[32 * n : 32 * n + 32]
 
     for phase, ref in enumerate((r1, r2, r2, r1)):
         pltpu.make_async_copy(ref, ref, ex_send.at[phase]).wait()
@@ -362,13 +363,13 @@
     f_copy.wait()
 
 
-def iterate_kernel(g_ref, first_ref, f_hbm, proj_hbm, scores_hbm, gf, gh, gm, gl, tt, fs, sc, pj, f_sem, o_sem, p_sem):
+def iterate_kernel(g0, g1, g2, g3, first_ref, f_hbm, proj_hbm, scores_hbm, gf, gh, gm, gl, tt, fs, sc, pj, f_sem, o_sem, p_sem):
     f_copy = pltpu.make_async_copy(f_hbm, fs, f_sem)
     f_copy.start()
 
     gf[BP:512, :] = jnp.zeros((512 - BP, 512), F32)
     for t, (rt, ct) in enumerate(LOWER):
-        tile = g_ref[t]
+        tile = (g0, g1, g2, g3)[t // 32][t % 32]
         if rt == 53 or ct == 3:
             ri, ci = iotas((8, 128))
             tile = jnp.where((ri + 8 * rt < BANDS) & (ci + 128 * ct < BANDS), tile, 0.0)
@@ -432,7 +433,7 @@
             jax.ShapeDtypeStruct((BANDS, BANDS), F32),
             jax.ShapeDtypeStruct((RANK * ROWS, COLS), F32),
         ),
-        in_specs=[vmem, vmem, hbm],
+        in_specs=[*[vmem] * 5, hbm],
         out_specs=(hbm, hbm),
         scratch_shapes=[
             pltpu.VMEM((512, 512), F32),
@@ -447,8 +448,8 @@
             dma((3,)),
             dma,
         ],
-        compiler_params=pltpu.CompilerParams(vmem_limit_bytes=53 * 2**20),
-    )(tiles, begin, features)
+        compiler_params=pltpu.CompilerParams(vmem_limit_bytes=54528 * 1024),
+    )(*tiles, begin, features)
 
 
 def first(counts, x, start):
@@ -459,11 +460,11 @@
         features_kernel,
         out_shape=(
             jax.ShapeDtypeStruct((BP, ROWS * COLS), BF16),
-            jax.ShapeDtypeStruct((128, 8, 128), F32),
+            *[jax.ShapeDtypeStruct((32, 8, 128), F32)] * 4,
             jax.ShapeDtypeStruct((RANK, 512), F32),
         ),
         in_specs=[pl.BlockSpec(memory_space=pltpu.SMEM), hbm, hbm],
-        out_specs=(hbm, vmem, vmem),
+        out_specs=(hbm, *[vmem] * 5),
         scratch_shapes=[
             pltpu.VMEM((ROWS * (BP + 2), COLS), BF16),
             pltpu.VMEM((HR, COLS), BF16),
@@ -494,14 +495,14 @@
             dma,
         ],
         compiler_params=pltpu.CompilerParams(
-            collective_id=0, has_side_effects=True, vmem_limit_bytes=53 * 2**20
+            collective_id=0, has_side_effects=True, vmem_limit_bytes=54528 * 1024
         ),
     )(counts, x, start.T)
 
 
 def on_device(radiance, counts, start):
     x = radiance.reshape(BANDS * ROWS, COLS)
-    features, tiles, begin = first(counts, x, start)
+    features, *tiles, begin = first(counts, x, start)
     projector, scores = second(tiles, begin, features)
     return projector, scores.reshape(1, RANK, ROWS, COLS)
 

time: 56.4 us -> 55.5 us (0.984)
  local copies, waits for them, and re-layouts: 0.9 us -> 0 us
    unnamed x2 -> x0, local copies, waits for them, and re-layouts: 0.9 us -> none
where the time goes in v8:
time: 55.5 us; the launch traced here: 55.4 us
  Pallas kernels  54.1 us (97%)
  between operations  1.28 us (2%)
    pallas_call x1, Pallas kernels, first(): pl.pallas_call(features_kernel, out_shape=(jax.ShapeDtypeStruct((BP, ROWS...  41.8 us
    pallas_call x1, Pallas kernels, second(): pl.pallas_call(iterate_kernel, out_shape=(jax.ShapeDtypeStruct((BANDS, BA...  12.3 us

profile of v8, /device:TPU:1, one launch (start us, length us, event | category | flops | bytes accessed | tf_op | source)
XLA Modules:
  0.0 55.4 jit_solution(10602239304944862584)
XLA Ops:
  1.3 41.8 %shard_map.50 = (bf16[432,6144]{1,0:T(8,128)(2,1)}, f32[32,8,128]{2,1,0:T(8,128)S(1)}, f32[32,8,128]{2,1,0:T(8,128)S(1)}, f32[32,8,128]{2,1,0:T(8,128)S(1)}, f32...) custom-call(s32[1,1]{1,0:T(1,128)S(6)} %copy.5.counts_ref, bf16[6800,384]{1,0:T(8,128)(2,1)} %bitcast.3, f32[64,425]{1,0:T(8,128)} %bitcast.4), custom_call_target="tpu_custom_call" | custom-call | tf_op jit(solution)/shard_map/pallas_call | solution.py:459
  43.0 12.3 %shard_map.51 = (f32[425,425]{1,0:T(8,128)}, f32[1024,384]{1,0:T(8,128)}) custom-call(f32[32,8,128]{2,1,0:T(8,128)S(1)} %get-tuple-element.10.g0, f32[32,8,128]{2,1,0:T(8,128)S(1)} %get-tuple-element.11.g1, f32[32,8,128]{2,1,0:T(8,128)S(1)} %get-tuple-element.12.g2, f32[32,8,128]{2,1,0:T(8,128)S(1)} %get-tuple-element.13.g3, ...), custom_call_target="tpu_custom_call" | custom-call | tf_op jit(solution)/shard_map/pallas_call | solution.py:430

commit v9 on v8

--- a/solution.py
+++ b/solution.py
@@ -259,17 +259,16 @@
     for device in on_axis[2]:
         pl.semaphore_signal(line_sem.at[1], inc=1, device_id=device, device_id_type=MESH)
 
-    def outer(lo, hi):
-        a = fs[:, lo:hi]
+    def outer(a):
         left = lax.dot_general(a, a[0:256], NT, preferred_element_type=F32)
         right = lax.dot_general(a[256:BP], a[256:BP], NT, preferred_element_type=F32)
         return left, right
 
-    left, right = outer(2 * COLS, 6 * COLS)
+    left, right = outer(fs[:, 2 * COLS : 6 * COLS])
     gs[:, 0:256] = left
     gs[256:BP, 256:BP] = right
     for k in (6, 10):
-        left, right = outer(k * COLS, (k + 4) * COLS)
+        left, right = outer(fs[:, k * COLS : (k + 4) * COLS])
         gs[:, 0:256] += left
         gs[256:BP, 256:BP] += right
 
@@ -308,10 +307,9 @@
     f_copy = pltpu.make_async_copy(fs, f_hbm, f_sem)
     f_copy.start()
 
-    for k in (0, 14):
-        left, right = outer(k * COLS, (k + 2) * COLS)
-        gs[:, 0:256] += left
-        gs[256:BP, 256:BP] += right
+    left, right = outer(jnp.concatenate([fs[:, 0 : 2 * COLS], fs[:, 14 * COLS : 16 * COLS]], axis=1))
+    gs[:, 0:256] += left
+    gs[256:BP, 256:BP] += right
 
     for t, (rt, ct) in enumerate(LOWER):
         pk[t] = gs[8 * rt : 8 * rt + 8, 128 * ct : 128 * ct + 128]

time: 55.5 us -> 55.6 us (level)
  no operation moved by 1% of the time
where the time goes in v9:
time: 55.6 us; the launch traced here: 55.5 us
  Pallas kernels  54.2 us (97%)
  between operations  1.28 us (2%)
    pallas_call x1, Pallas kernels, first(): pl.pallas_call(features_kernel, out_shape=(jax.ShapeDtypeStruct((BP, ROWS...  41.8 us
    pallas_call x1, Pallas kernels, second(): pl.pallas_call(iterate_kernel, out_shape=(jax.ShapeDtypeStruct((BANDS, BA...  12.4 us

profile of v9, /device:TPU:1, one launch (start us, length us, event | category | flops | bytes accessed | tf_op | source)
XLA Modules:
  0.0 55.5 jit_solution(12984557977666794361)
XLA Ops:
  1.3 41.8 %shard_map.50 = (bf16[432,6144]{1,0:T(8,128)(2,1)}, f32[32,8,128]{2,1,0:T(8,128)S(1)}, f32[32,8,128]{2,1,0:T(8,128)S(1)}, f32[32,8,128]{2,1,0:T(8,128)S(1)}, f32...) custom-call(s32[1,1]{1,0:T(1,128)S(6)} %copy.5.counts_ref, bf16[6800,384]{1,0:T(8,128)(2,1)} %bitcast.3, f32[64,425]{1,0:T(8,128)} %bitcast.4), custom_call_target="tpu_custom_call" | custom-call | tf_op jit(solution)/shard_map/pallas_call | solution.py:457
  43.1 12.4 %shard_map.51 = (f32[425,425]{1,0:T(8,128)}, f32[1024,384]{1,0:T(8,128)}) custom-call(f32[32,8,128]{2,1,0:T(8,128)S(1)} %get-tuple-element.10.g0, f32[32,8,128]{2,1,0:T(8,128)S(1)} %get-tuple-element.11.g1, f32[32,8,128]{2,1,0:T(8,128)S(1)} %get-tuple-element.12.g2, f32[32,8,128]{2,1,0:T(8,128)S(1)} %get-tuple-element.13.g3, ...), custom_call_target="tpu_custom_call" | custom-call | tf_op jit(solution)/shard_map/pallas_call | solution.py:428
